TPU v7x, 512 devices: a whole 4x4x16 slice. The times are simulated.
512 devices in a mesh: row: 64 (over x, z), col: 8 (over y, core).
Axes of the slice: x: 4, y: 4, z: 16, core: 2. Of those that a mesh axis runs over, the one named last changes fastest.
Arguments:
- momentum: float32 [8192, 26624], P('row', 'col')
- gradient: bfloat16 [8192, 26624], P('row', 'col'), may hold values from -6 to 6
- factor: float32 [26624, 256], P(('col', 'row'))
Outputs:
- momentum_out: float32 [8192, 26624], P('row', 'col')
- weight_update: bfloat16 [8192, 26624], P('row', 'col')
- factor_out: float32 [26624, 256], P(('col', 'row'))
All inputs are finite; a program needn't handle non-finite values.
Results may differ from a plain program's by a relative error of at most 0.0013.
Values sent between devices are 32-bit elements; how exact they have to be, the bound alone decides.
A program may use at most 64 MiB of HBM per device.

v0:
```python
import math

import jax
import jax.numpy as jnp
from jax import lax
from jax.sharding import PartitionSpec as P

N_COLS = 26624


HIGHEST = lax.Precision.HIGHEST
MOMENTUM_KEEP = 0.8
STEP_SIZE = 0.3
EPSILON = 1e-06


def unit_columns(left_panel, gram_matrix):
    lower_factor = jnp.linalg.cholesky(gram_matrix)
    return lax.linalg.triangular_solve(
        lower_factor, left_panel, left_side=False, lower=True, transpose_a=True
    )


def self_gram(matrix):
    return jnp.dot(matrix.T, matrix, precision=HIGHEST, preferred_element_type=jnp.float32)


def transposed_product(columns, left_basis):
    return lax.dot_general(
        columns,
        left_basis,
        (((0,), (0,)), ((), ())),
        precision=HIGHEST,
        preferred_element_type=jnp.float32,
    )


def shards(momentum, gradient, factor):
    buffer = momentum + gradient.astype(jnp.float32)
    rows_here = buffer.shape[0]
    rank_width = factor.shape[1]
    factor_here = factor.shape[0]
    row_count = lax.axis_size("row")
    partial_panel = jnp.dot(
        buffer,
        lax.all_gather(factor, "row", axis=0, tiled=True),
        precision=HIGHEST,
        preferred_element_type=jnp.float32,
    )
    left_panel = lax.psum(partial_panel, "col")
    gram_matrix = lax.psum(self_gram(left_panel), "row")
    left_basis = unit_columns(left_panel, gram_matrix)
    right_factor = lax.psum(transposed_product(buffer, left_basis), "row")
    squares = lax.psum(jnp.sum(right_factor * right_factor, axis=0), "col")
    column_rms = jnp.sqrt(squares / N_COLS + EPSILON)
    full_factor = right_factor / column_rms
    factor_out = lax.dynamic_slice_in_dim(
        full_factor, lax.axis_index("row") * factor_here, factor_here, 0
    )
    feedback = jnp.dot(
        left_basis, right_factor.T, precision=HIGHEST, preferred_element_type=jnp.float32
    )
    momentum_out = buffer - (1.0 - MOMENTUM_KEEP) * feedback
    update = jnp.dot(
        left_basis, full_factor.T, precision=HIGHEST, preferred_element_type=jnp.float32
    )
    scale_factor = STEP_SIZE * math.sqrt(rows_here * row_count / rank_width)
    weight_update = (-scale_factor * update).astype(jnp.bfloat16)
    return (momentum_out, weight_update, factor_out)


def solution(mesh):
    placed = (P("row", "col"), P("row", "col"), P(("col", "row"), None))
    return jax.shard_map(
        shards,
        mesh=mesh,
        in_specs=placed,
        out_specs=(P("row", "col"), P("row", "col"), P(("col", "row"), None)),
        check_vma=False,
    )
```

profile of v0, /device:TPU:1, one launch (start us, length us, event | category | flops | bytes accessed | tf_op | source)
XLA Modules:
  0.0 887.5 jit_solution(5916730785001772341)
XLA Ops:
  7.2 0.7 all-gather.3.cloned.1.call-update
  8.0 144.3 %all-gather.3.cloned.1.call-done = f32[64,52,256]{2,1,0:T(8,128)} async-done(((f32[1,52,256]{2,1,0:T(8,128)}), f32[64,52,256]{2,1,0:T(8,128)}) %all-gather.3.cloned.1.call-update) | async-done | bytes 3407888 | tf_op jit(solution)/shard_map/all_gather | solution.py:46
  152.3 4.6 reshape.44
  157.0 4.4 fusion.3
  161.5 77.1 %all-reduce.5.cloned.1.call-done = f32[128,256]{1,0:T(8,128)} async-done(((f32[128,256]{1,0:T(8,128)}), f32[128,256]{1,0:T(8,128)}) %all-reduce.5.cloned.1.call-update) | async-done | bytes 131088 | tf_op jit(solution)/shard_map/psum | solution.py:50
  238.5 2.1 fusion.16
  240.6 0.2 all-reduce.9.cloned.1.call-start
  240.9 255.3 %all-reduce.7.cloned.1.call-done = f32[256,256]{0,1:T(8,128)} async-done(((f32[256,256]{0,1:T(8,128)}), f32[256,256]{0,1:T(8,128)}) %all-reduce.7.cloned.1.call-update) | async-done | bytes 262160 | tf_op jit(solution)/shard_map/psum | solution.py:51
  496.2 1.1 copy.11
  497.3 1.0 fusion.4
  498.4 11.7 %cholesky.50 = f32[128,128]{1,0:T(8,128)S(1)} custom-call(f32[128,128]{1,0:T(8,128)S(1)} %cholesky.118), custom_call_target="Cholesky" | custom-call | tf_op jit(solution)/shard_map/jit(cholesky)/cholesky | solution.py:18
  510.1 9.8 %custom-call.14 = f32[1,128,128]{1,2,0:T(8,128)S(1)} custom-call(f32[1,128,128]{2,1,0:T(8,128)S(1)} %get-tuple-element.24), custom_call_target="InvertDiagBlocksLowerTriangular" | custom-call | tf_op jit(solution)/shard_map/jit(cholesky)/cholesky | solution.py:18
  520.2 0.3 convolution_subtract_fusion.1
  520.4 11.7 %cholesky.105 = f32[128,128]{1,0:T(8,128)S(1)} custom-call(f32[128,128]{1,0:T(8,128)S(1)} %convolution_subtract_fusion.1), custom_call_target="Cholesky" | custom-call | tf_op jit(solution)/shard_map/jit(cholesky)/cholesky | solution.py:18
  532.2 0.7 compare_reduce_fusion
  534.4 5.5 while.1
  534.6 0.6 fusion.27
  535.2 2.1 bitcast_dynamic-update-slice_fusion.2
  537.2 0.6 fusion.27
  537.8 2.1 bitcast_dynamic-update-slice_fusion.2
  539.9 20.5 %custom-call.15 = f32[2,128,128]{1,2,0:T(8,128)S(1)} custom-call(f32[2,128,128]{2,1,0:T(8,128)} %get-tuple-element.10), custom_call_target="InvertDiagBlocksLowerTriangular" | custom-call | tf_op jit(solution)/shard_map/triangular_solve | solution.py:19
  560.4 0.3 fusion.7
  560.7 0.3 convolution_subtract_fusion
  561.0 0.3 fusion.5
  561.3 4.6 fusion.2
  565.9 281.1 %all-reduce.9.cloned.1.call-done = f32[3328,256]{1,0:T(8,128)} async-done(((f32[3328,256]{1,0:T(8,128)}), f32[3328,256]{1,0:T(8,128)}) %all-reduce.9.cloned.1.call-update) | async-done | bytes 3407888 | tf_op jit(solution)/shard_map/psum | solution.py:53
  847.0 2.6 multiply_reduce_fusion
  849.6 21.0 %psum.31 = f32[256]{0:T(256)S(1)} all-reduce(f32[256]{0:T(256)S(1)} %multiply_reduce_fusion), channel_id=1, replica_groups=mesh['row'=64,'col'=8] {'col'}, use_global_device_ids=true, to_apply=%region_8.9 | all-reduce | flops 256 | bytes 2048 | tf_op jit(solution)/shard_map/psum | solution.py:54
  870.6 0.2 broadcast_divide_fusion
  870.8 4.6 fusion.1
  875.4 0.6 constant_dynamic-slice_fusion.1
  876.1 4.9 fusion
  (30 shorter events, 0.6 us)
Async XLA Ops:
  7.2 145.2 %all-gather.3.cloned.1.call-start = ((), (), s32[]{:S(2)}) async-start(), calls=%async_computation.3 | async-start | bytes 3727360 | tf_op jit(solution)/shard_map/all_gather | solution.py:46
  7.9 149.1 %copy-start.1 = (f32[128,3328]{1,0:T(8,128)S(1)}, f32[128,3328]{1,0:T(8,128)}, u32[]{:S(2)}) copy-start(f32[128,3328]{1,0:T(8,128)} %param.3) | copy-start | bytes 5111812
  7.9 149.1 %copy-start.3 = (bf16[128,3328]{1,0:T(8,128)(2,1)S(1)}, bf16[128,3328]{1,0:T(8,128)(2,1)}, u32[]{:S(2)}) copy-start(bf16[128,3328]{1,0:T(8,128)(2,1)} %param.4) | copy-start | bytes 2555908
  7.9 230.6 %all-reduce.5.cloned.1.call-start = ((), (), s32[]{:S(2)}) async-start(), calls=%async_computation | async-start | bytes 262144 | tf_op jit(solution)/shard_map/psum | solution.py:50
  161.4 334.8 %all-reduce.7.cloned.1.call-start = ((), (), s32[]{:S(2)}) async-start(), calls=%async_computation.1 | async-start | bytes 524288 | tf_op jit(solution)/shard_map/psum | solution.py:51
  240.6 606.4 %all-reduce.9.cloned.1.call-start = ((), (), s32[]{:S(2)}) async-start(), calls=%async_computation.2 | async-start | bytes 6815744 | tf_op jit(solution)/shard_map/psum | solution.py:53
  497.3 63.0 %copy-start.5 = (f32[128,256]{1,0:T(8,128)S(1)}, f32[128,256]{1,0:T(8,128)}, u32[]{:S(2)}) copy-start(f32[128,256]{1,0:T(8,128)} %all-reduce.5.cloned.1.call-done) | copy-start | bytes 393220
  847.0 23.6 %copy-start = (f32[3328,256]{1,0:T(8,128)S(1)}, f32[3328,256]{1,0:T(8,128)}, u32[]{:S(2)}) copy-start(f32[3328,256]{1,0:T(8,128)} %all-reduce.9.cloned.1.call-done) | copy-start | bytes 10223620
  870.8 5.3 copy-start.2
  870.8 5.2 copy-start.4
Sparse Core Ops, SparseCore 0:
  10.9 141.3 all-gather.2
  161.5 76.9 all-reduce.4
  242.9 253.2 all-reduce.6
  566.1 280.9 all-reduce.8
where the time goes:
time: 888 us
  waiting for transfers between devices  759 us (85%)
  other arithmetic  58.4 us (7%)
  matrix products  22 us (2%)
  blocking collectives  21 us (2%)
  between operations  15.3 us (2%)
  local copies, waits for them, and re-layouts  11.8 us (1%)
    psum x1, waiting for transfers between devices, shards(): right_factor = lax.psum(transposed_product(buffer, left_basis), 'row')  281 us
    psum x1, waiting for transfers between devices, shards(): gram_matrix = lax.psum(self_gram(left_panel), 'row')  255 us
    all_gather x1, waiting for transfers between devices, shards(): lax.all_gather(factor, 'row', axis=0, tiled=True)  144 us
    psum x1, waiting for transfers between devices, shards(): left_panel = lax.psum(partial_panel, 'col')  77.1 us
    another operation x6, other arithmetic, unit_columns(): lower_factor = jnp.linalg.cholesky(gram_matrix)  34 us
    psum x1, blocking collectives, shards(): squares = lax.psum(jnp.sum(right_factor * right_factor, axis=0), 'col')  21 us
    another operation x3, other arithmetic, unit_columns(): lax.linalg.triangular_solve(lower_factor, left_panel, left_side=False, lo...  20.5 us
  transfers between devices with their start and end apart: 4, of which 4 were waited for; matrix products, arithmetic and copies ran while one was open for 0% of the time, Pallas kernels for 0%

commit v1 on v0

v1 whole, which is shorter than its diff:
```python
import functools
import math

import jax
import jax.numpy as jnp
from jax import lax
from jax.experimental import pallas as pl
from jax.experimental.pallas import tpu as pltpu
from jax.sharding import PartitionSpec as P

HIGHEST = lax.Precision.HIGHEST
MOMENTUM_KEEP = 0.8
STEP_SIZE = 0.3
EPSILON = 1e-06
F32 = jnp.float32
BF16 = jnp.bfloat16

NX, NZ = 4, 16
NC = 8
CH = 104
CA = 64
CB = CH - CA
ROWS, COLS, RANK = 128, 3328, 256
BLK = 256
NBLK = COLS // BLK
NB = 32


def split(value):
    high = value.astype(BF16)
    return high, (value - high.astype(F32)).astype(BF16)


def dot(a, b, dims=((1,), (0,))):
    return lax.dot_general(a, b, (dims, ((), ())), preferred_element_type=F32)


def dot3(a, b, dims=((1,), (0,))):
    return dot(a[0], b[0], dims) + (dot(a[0], b[1], dims) + dot(a[1], b[0], dims))


def dot6(a, b, dims=((1,), (0,))):
    return lax.dot_general(a, b, (dims, ((), ())), precision=HIGHEST, preferred_element_type=F32)


class Links:
    def __init__(self, ssem, rsem):
        self.ssem, self.rsem = ssem, rsem
        self.r, self.c = lax.axis_index("row"), lax.axis_index("col")
        self.x, self.z = self.r // NZ, self.r % NZ

    def mod(self, value, n):
        return lax.rem(value + 4 * n, n)

    def at_x(self, d):
        return {"row": self.mod(self.x + d, NX) * NZ + self.z, "col": self.c}

    def at_z(self, d):
        return {"row": self.x * NZ + self.mod(self.z + d, NZ), "col": self.c}

    def at_c(self, d):
        return {"row": self.r, "col": self.mod(self.c + d, NC)}

    def at_q(self, d):
        return {"row": self.x * NZ + (self.z // 4) * 4 + lax.rem(self.z + d, 4), "col": self.c}

    def copy(self, src, dst, recv, device, slot=0):
        return pltpu.make_async_remote_copy(
            src_ref=src, dst_ref=dst, send_sem=self.ssem.at[slot], recv_sem=recv,
            device_id=device, device_id_type=pl.DeviceIdType.MESH)

    def send(self, src, dst, recv, device, slot):
        self.copy(src, dst, recv, device, slot).start()

    def recv(self, dst, sem):
        self.copy(dst, dst, sem, self.at_x(1)).wait_recv()

    def sent(self, ref, slot):
        self.copy(ref, ref, self.rsem, self.at_x(1), slot).wait_send()

    def greet(self, peers):
        barrier = pltpu.get_barrier_semaphore()
        for peer in peers:
            pl.semaphore_signal(barrier, inc=1, device_id=peer, device_id_type=pl.DeviceIdType.MESH)
        return lambda: pl.semaphore_wait(barrier, len(peers))


def block(b):
    return pl.ds(pl.multiple_of(b * BLK, BLK), BLK)


def split_rows(ref, b):
    parts = [split(ref[pl.ds(2 * BLK * b + h, BLK, stride=2), :]) for h in (0, 1)]
    return tuple(jnp.concatenate(p, axis=1) for p in zip(*parts))


def gather(t, buf4, slot, sems, work):
    agaz, agax, agbx, agbz = sems
    x, z, own, other = t.x, t.z, t.x // 2, 1 - t.x // 2
    mod, at_x, at_z, send, recv = t.mod, t.at_x, t.at_z, t.send, t.recv

    def piece(xi, zi, lo=0, size=CA):
        return buf4.at[xi, zi, pl.ds(lo, size)]

    def pair(g, zi):
        return buf4.at[pl.ds(2 * g, 2), zi, pl.ds(CA, CB)]

    def side(zi, k):
        send(piece(x, zi), piece(x, zi), agax.at[0, k], at_x(1), slot)
        send(piece(x, zi), piece(x, zi), agax.at[1, k], at_x(-1), slot)

    def forward(zi, k):
        left, right = mod(x - 1, NX), mod(x + 1, NX)
        recv(piece(left, zi), agax.at[0, k])
        send(piece(left, zi, 0, CA // 2), piece(left, zi, 0, CA // 2), agax.at[2, k], at_x(1), slot)
        recv(piece(right, zi), agax.at[1, k])
        send(piece(right, zi, CA // 2, CA // 2), piece(right, zi, CA // 2, CA // 2), agax.at[3, k], at_x(-1), slot)

    def finish(zi, k):
        far = mod(x + 2, NX)
        recv(piece(far, zi, 0, CA // 2), agax.at[2, k])
        recv(piece(far, zi, CA // 2, CA // 2), agax.at[3, k])

    for d in (1, 2, 3):
        send(piece(x, z, CA, CB), piece(x, z, CA, CB), agbx.at[d], at_x(d), slot)
    send(piece(x, z), piece(x, z), agaz.at[0, 1], at_z(1), slot)
    send(piece(x, z), piece(x, z), agaz.at[1, 1], at_z(-1), slot)
    side(z, 0)
    for d in (1, 2, 3):
        recv(piece(mod(x - d, NX), z, CA, CB), agbx.at[d])
    for i, g in enumerate((own, other)):
        send(pair(g, z), pair(g, z), agbz.at[0, i, 1], at_z(1), slot)
        send(pair(g, z), pair(g, z), agbz.at[1, i, 1], at_z(-1), slot)

    def step(s, carry):
        zr, zl = mod(z - s, NZ), mod(z + s, NZ)
        recv(piece(x, zr), agaz.at[0, s])
        send(piece(x, zr), piece(x, zr), agaz.at[0, s + 1], at_z(1), slot)
        recv(piece(x, zl), agaz.at[1, s])

        @pl.when(s < 7)
        def _():
            send(piece(x, zl), piece(x, zl), agaz.at[1, s + 1], at_z(-1), slot)

        side(zr, s)
        side(zl, 8 + s)
        for i, g in enumerate((own, other)):
            recv(pair(g, zl), agbz.at[1, i, s])
            send(pair(g, zl), pair(g, zl), agbz.at[1, i, s + 1], at_z(-1), slot)
            recv(pair(g, zr), agbz.at[0, i, s])

            @pl.when(s < 7)
            def _():
                send(pair(g, zr), pair(g, zr), agbz.at[0, i, s + 1], at_z(1), slot)

        forward(mod(z - s + 1, NZ), s - 1)

        @pl.when(s > 1)
        def _():
            forward(mod(z + s - 1, NZ), 7 + s)

        work(s)
        return carry

    lax.fori_loop(1, 8, step, 0)
    far = mod(z + 8, NZ)
    recv(piece(x, far), agaz.at[0, 8])
    side(far, 8)
    forward(mod(z - 7, NZ), 7)
    forward(mod(z + 7, NZ), 15)
    for i, g in enumerate((own, other)):
        recv(pair(g, far), agbz.at[1, i, 8])
    forward(far, 8)

    def last(k, carry):
        finish(mod(jnp.where(k > 8, z + k - 8, z - k), NZ), k)
        return carry

    lax.fori_loop(0, 16, last, 0)
    t.sent(buf4.reshape(NX * NZ * CH, 128).at[pl.ds(0, 6552)], slot)


def panel_kernel(mom, grad, fac, panel, thi, tlo, momv, gradv, bhi, blo, gat, ppart, precv,
                 lsem, ssem, agaz, agax, agbx, agbz, psem):
    t = Links(ssem, agbx.at[0])
    r, c, mod, at_c, send, recv, sent = t.r, t.c, t.mod, t.at_c, t.send, t.recv, t.sent
    loads = (pltpu.make_async_copy(mom, momv, lsem.at[0]), pltpu.make_async_copy(grad, gradv, lsem.at[1]))
    for load in loads:
        load.start()
    greeted = t.greet([t.at_x(d) for d in (1, 2, 3)] + [at_c(d) for d in range(1, NC)] + [t.at_z(1), t.at_z(-1)])
    gat2 = gat.reshape(NX * NZ * CH, 128)

    gat2[pl.ds(CH * r, CH // 2, stride=2), :] = fac[:, :128]
    gat2[pl.ds(CH * r + 1, CH // 2, stride=2), :] = fac[:, 128:]
    greeted()

    def prepare(b):
        at = block(b)
        value = momv[:, at] + gradv[:, at].astype(F32)
        high, low = split(value)
        bhi[:, at], blo[:, at] = high, low
        high, low = split(value.T)
        thi[at, :], tlo[at, :] = high, low

    def prepare_step(s):
        @pl.when(s == 1)
        def _():
            for load in loads:
                load.wait()

        prepare(2 * s - 2)

        @pl.when(s < 7)
        def _():
            prepare(2 * s - 1)

    gather(t, gat, 0, (agaz, agax, agbx, agbz), prepare_step)

    def panel_step(b, total):
        at = block(b)
        return total + dot3((bhi[:, at], blo[:, at]), split_rows(gat2, b))

    total = lax.fori_loop(0, NBLK, panel_step, jnp.zeros((ROWS, RANK), F32))
    ppart[...] = total.reshape(NC, ROWS // NC, RANK)
    for d in range(1, NC):
        peer = mod(c + d, NC)
        send(ppart.at[peer], precv.at[d], psem.at[0, d], at_c(d), 1)
    mine = ppart[c]
    for d in range(1, NC):
        recv(precv.at[d], psem.at[0, d])
        mine = mine + precv[d]
    panel[c] = mine
    for d in range(1, NC):
        send(panel.at[c], panel.at[c], psem.at[1, d], at_c(d), 1)
    for d in range(1, NC):
        recv(panel.at[mod(c - d, NC)], psem.at[1, d])
    sent(gat2.at[pl.ds(0, 14 * 32)], 1)


def factor_kernel(panel, thi, tlo, rfh, rfl, basis, update, ownf,
                  part, red, xh, xf, za, zb, xb, gram, g0, g1, g2, g3, g4, aw, rfhv, rflv, sq, sqr,
                  ssem, agaz, agax, agbx, agbz, rsx, rsza, rszb, rsxb, gsem, qsem, osem, *, n_cols, scale):
    links = Links(ssem, agbx.at[0])
    r, c, x, z, mod = links.r, links.c, links.x, links.z, links.mod
    at_x, at_z, at_c, at_q = links.at_x, links.at_z, links.at_c, links.at_q
    send, recv, sent = links.send, links.recv, links.sent
    greeted = links.greet([at_x(d) for d in (1, 2, 3)] + [at_c(d) for d in range(1, NC)]
                      + [at_z(d) for d in (1, -1, 4, 8, 12)] + [at_q(d) for d in (1, 2, 3)])
    part2 = part.reshape(NX * NZ * CH, 128)
    red2 = red.reshape(NX * NZ * CH, 128)
    own, other = x // 2, 1 - x // 2

    left = panel[...]
    gram[...] = dot6(left.T, left)
    greeted()
    for d in (1, 2, 3):
        src = gram.at[pl.ds(pl.multiple_of(32 * c + 8 * mod(x + d, NX), 8), 8)]
        send(src, g0.at[d], gsem.at[0, d], at_x(d), 2)

    def gram_0():
        total = gram[pl.ds(pl.multiple_of(32 * c + 8 * x, 8), 8), :]
        for d in (1, 2, 3):
            recv(g0.at[d], gsem.at[0, d])
            total = total + g0[d]
        g1[0] = total
        for d in (1, 2, 3):
            send(g1.at[0], g1.at[d], gsem.at[1, d], at_q(d), 2)

    def gram_1():
        total = g1[0]
        for d in (1, 2, 3):
            recv(g1.at[d], gsem.at[1, d])
            total = total + g1[d]
        g2[0] = total
        for d in (1, 2, 3):
            send(g2.at[0], g2.at[d], gsem.at[2, d], at_z(4 * d), 2)

    def gram_2():
        total = g2[0]
        for d in (1, 2, 3):
            recv(g2.at[d], gsem.at[2, d])
            total = total + g2[d]
        g3[x] = total
        for d in (1, 2, 3):
            send(g3.at[x], g3.at[x], gsem.at[3, d], at_x(d), 2)

    def gram_3():
        for d in (1, 2, 3):
            recv(g3.at[mod(x - d, NX)], gsem.at[3, d])
        g4[c] = g3[...]
        for d in range(1, NC):
            send(g4.at[c], g4.at[c], gsem.at[4, d], at_c(d), 3)

    def gram_4():
        for d in range(1, NC):
            recv(g4.at[mod(c - d, NC)], gsem.at[4, d])
        aw[...] = g4[...].reshape(RANK, RANK)
        sent(gram.at[pl.ds(0, 96)], 2)
        sent(g4.at[pl.ds(0, NC - 1)], 3)

    lp = split(left)

    def term_step(b, carry):
        at = block(b)
        h = dot3((thi[at, :], tlo[at, :]), lp)
        part2[pl.ds(2 * BLK * b, BLK, stride=2), :] = h[:, :128]
        part2[pl.ds(2 * BLK * b + 1, BLK, stride=2), :] = h[:, 128:]
        return carry

    lax.fori_loop(0, NBLK, term_step, 0)

    xr, xl, xo = mod(x + 1, NX), mod(x - 1, NX), mod(x + 2, NX)
    half = CA // 2

    def send_half(zi, k):
        send(part.at[xo, zi, pl.ds(0, half)], xh.at[0, k], rsx.at[0, k], at_x(1), 4)
        send(part.at[xo, zi, pl.ds(half, half)], xh.at[1, k], rsx.at[1, k], at_x(-1), 4)

    def send_full(zi, k):
        recv(xh.at[0, k], rsx.at[0, k])
        part[xr, zi, :half, :] += xh[0, k]
        send(part.at[xr, zi, pl.ds(0, CA)], xf.at[0, k], rsx.at[2, k], at_x(1), 4)
        recv(xh.at[1, k], rsx.at[1, k])
        part[xl, zi, half:CA, :] += xh[1, k]
        send(part.at[xl, zi, pl.ds(0, CA)], xf.at[1, k], rsx.at[3, k], at_x(-1), 4)

    def take_full(zi, k):
        recv(xf.at[0, k], rsx.at[2, k])
        recv(xf.at[1, k], rsx.at[3, k])
        part[x, zi, :CA, :] += xf[0, k] + xf[1, k]

    def to_right(t):
        return mod(z + 8 - t, NZ)

    def to_left(t):
        return mod(z - 7 + t, NZ)

    for t in (0, 1):
        send_half(to_right(t), t)
        send_half(to_left(t), 8 + t)
    send_full(to_right(0), 0)
    send_full(to_left(0), 8)

    def reduce_step(t, carry):
        @pl.when(t < 6)
        def _():
            send_half(to_right(t + 2), t + 2)

        @pl.when(t < 6)
        def _():
            send_half(to_left(t + 2), 10 + t)

        @pl.when(t < 7)
        def _():
            send_full(to_right(t + 1), t + 1)

        @pl.when(t < 7)
        def _():
            send_full(to_left(t + 1), 9 + t)

        take_full(to_right(t), t)

        @pl.when(t > 0)
        def _():
            recv(za.at[0, t], rsza.at[0, t])
            part[x, to_right(t), :CA, :] += za[0, t]

        send(part.at[x, to_right(t), pl.ds(0, CA)], za.at[0, t + 1], rsza.at[0, t + 1], at_z(1), 4)

        @pl.when(t < 7)
        def _():
            take_full(to_left(t), 8 + t)

            @pl.when(t > 0)
            def _():
                recv(za.at[1, t], rsza.at[1, t])
                part[x, to_left(t), :CA, :] += za[1, t]

            send(part.at[x, to_left(t), pl.ds(0, CA)], za.at[1, t + 1], rsza.at[1, t + 1], at_z(-1), 4)

        bl, br = mod(z - 8 + t, NZ), mod(z + 7 - t, NZ)
        for i, g in enumerate((other, own)):
            rows = pl.ds(2 * g, 2)

            @pl.when(t > 0)
            def _():
                recv(zb.at[1, i, t], rszb.at[1, i, t])
                part[rows, bl, CA:, :] += zb[1, i, t]

            send(part.at[rows, bl, pl.ds(CA, CB)], zb.at[1, i, t + 1], rszb.at[1, i, t + 1], at_z(-1), 4)

            @pl.when(t < 7)
            def _():
                @pl.when(t > 0)
                def _():
                    recv(zb.at[0, i, t], rszb.at[0, i, t])
                    part[rows, br, CA:, :] += zb[0, i, t]

                send(part.at[rows, br, pl.ds(CA, CB)], zb.at[0, i, t + 1], rszb.at[0, i, t + 1], at_z(1), 4)

        for when, stage in enumerate((gram_0, gram_1, gram_2, gram_3, gram_4)):
            pl.when(t == when)(stage)
        return carry

    lax.fori_loop(0, 8, reduce_step, 0)
    for i, g in enumerate((other, own)):
        recv(zb.at[1, i, 8], rszb.at[1, i, 8])
        recv(zb.at[0, i, 7], rszb.at[0, i, 7])
        part[pl.ds(2 * g, 2), z, CA:, :] += zb[1, i, 8] + zb[0, i, 7]
    for d in (1, 2, 3):
        send(part.at[mod(x + d, NX), z, pl.ds(CA, CB)], xb.at[d], rsxb.at[d], at_x(d), 4)
    take_full(z, 15)
    recv(za.at[0, 8], rsza.at[0, 8])
    recv(za.at[1, 7], rsza.at[1, 7])
    red[x, z, :CA, :] = part[x, z, :CA, :] + (za[0, 8] + za[1, 7])
    total = part[x, z, CA:, :]
    for d in (1, 2, 3):
        recv(xb.at[d], rsxb.at[d])
        total = total + xb[d]
    red[x, z, CA:, :] = total
    sent(part2.at[pl.ds(0, 6552)], 4)

    sub = lax.broadcasted_iota(jnp.int32, (NB, 128), 0)
    lane = lax.broadcasted_iota(jnp.int32, (NB, 128), 1)
    sub_w = lax.broadcasted_iota(jnp.int32, (NB, RANK), 0)
    lane_w = lax.broadcasted_iota(jnp.int32, (NB, RANK), 1)
    i_all = lax.broadcasted_iota(jnp.int32, (RANK, RANK), 0)
    j_all = lax.broadcasted_iota(jnp.int32, (RANK, RANK), 1)

    def factor_block(k):
        first = pl.multiple_of(NB * k, NB)
        rows = aw[pl.ds(first, NB), :]
        near = jnp.where(k < 4, rows[:, :128], rows[:, 128:])
        near = pltpu.roll(near, lax.rem(128 - NB * lax.rem(k, 4), 128), 1)
        e = jnp.where(lane < NB, near, jnp.where(lane - NB == sub, 1.0, 0.0))
        for j in range(0, NB, 4):
            cols = [jnp.broadcast_to(e[:, j + i:j + i + 1], (NB, 128)) for i in range(4)]
            pivots = [e[j + i:j + i + 1, :] for i in range(4)]
            for i in range(4):
                at = slice(j + i, j + i + 1)
                ratio = jnp.where(sub > j + i, cols[i] * (1.0 / cols[i][at, :]), 0.0)
                for m in range(i + 1, 4):
                    cols[m] = cols[m] - ratio * cols[m][at, :]
                    pivots[m] = pivots[m] - ratio[j + m:j + m + 1, :] * pivots[i]
                e = e - ratio * pivots[i]
        diagonal = jnp.sum(jnp.where(lane == sub, e, 0.0), axis=1, keepdims=True)
        inverse = (e * (1.0 / jnp.sqrt(diagonal)))[:, NB:2 * NB]
        here = (lane_w >= first) & (lane_w < first + NB)
        rows = jnp.where(here, jnp.where(lane_w - first == sub_w, 1.0, 0.0), rows)
        rows = dot6(inverse, rows)
        below = jnp.where(lane_w >= first + NB, rows, 0.0)
        done = (i_all >= first + NB) & (j_all >= first) & (j_all < first + NB)
        aw[...] = jnp.where(done, 0.0, aw[...]) - dot6(below.T, rows)
        aw[pl.ds(first, NB), :] = rows

    gather(links, red, 5, (agaz, agax, agbx, agbz), lambda s: factor_block(s - 1))
    factor_block(7)

    inverse = jnp.where(i_all >= j_all, aw[...], 0.0)
    nt = ((1,), (1,))
    inv = split(inverse)

    def right_step(b, squares):
        rf = dot3(split_rows(red2, b), inv, nt)
        rfhv[block(b), :], rflv[block(b), :] = split(rf)
        return squares + jnp.sum((rf * rf).reshape(BLK // 8, 8, RANK), axis=0)

    squares = lax.fori_loop(0, NBLK, right_step, jnp.zeros((8, RANK), F32))
    stores = (pltpu.make_async_copy(rfhv, rfh, osem.at[0]), pltpu.make_async_copy(rflv, rfl, osem.at[1]))
    for store in stores:
        store.start()
    sq[...] = squares
    for d in range(1, NC):
        send(sq, sqr.at[d], qsem.at[d], at_c(d), 6)
    left_basis = dot6(left, inverse, nt)
    halves = [red2[pl.ds(CH * r + h, CH // 2, stride=2), :] for h in (0, 1)]
    own_rf = dot6(jnp.concatenate(halves, axis=1), inverse, nt)
    for d in range(1, NC):
        recv(sqr.at[d], qsem.at[d])
        squares = squares + sqr[d]
    rms = jnp.sqrt(jnp.sum(squares, axis=0, keepdims=True) * (1.0 / n_cols) + EPSILON)
    ownf[...] = own_rf / rms
    basis[...] = left_basis * -(1.0 - MOMENTUM_KEEP)
    update[...] = left_basis * (-scale / rms)
    sent(gram.at[pl.ds(0, 8 * (NC - 1))], 6)
    for store in stores:
        store.wait()


def output_kernel(mom, grad, rfh, rfl, basis, update, ownf, momo, wupd, faco):
    nt = ((1,), (1,))
    right = (rfh[...], rfl[...])
    momo[...] = mom[...] + grad[...].astype(F32) + dot3(split(basis[...]), right, nt)
    wupd[...] = dot3(split(update[...]), right, nt).astype(BF16)

    @pl.when(pl.program_id(0) == 0)
    def _():
        faco[...] = ownf[...]


def shards(momentum, gradient, factor):
    rows = momentum.shape[0] * lax.axis_size("row")
    n_cols = momentum.shape[1] * lax.axis_size("col")
    scale = STEP_SIZE * math.sqrt(rows / factor.shape[1])
    dma, vmem, hbm = pltpu.SemaphoreType.DMA, pltpu.VMEM, pl.BlockSpec(memory_space=pl.ANY)
    inside = pl.BlockSpec(memory_space=pltpu.VMEM)
    shape = jax.ShapeDtypeStruct
    flat = vmem((NX, NZ, CH, 128), F32)
    gather_sems = [dma((2, 9)), dma((4, 16)), dma((4,)), dma((2, 2, 9))]
    rows16 = vmem((NC, ROWS // NC, RANK), F32)
    panel, thi, tlo = pl.pallas_call(
        panel_kernel,
        out_shape=(shape((NC, ROWS // NC, RANK), F32), shape((COLS, ROWS), BF16), shape((COLS, ROWS), BF16)),
        in_specs=[hbm, hbm, inside],
        out_specs=(inside, inside, inside),
        scratch_shapes=[
            vmem((ROWS, COLS), F32), vmem((ROWS, COLS), BF16), vmem((ROWS, COLS), BF16), vmem((ROWS, COLS), BF16),
            flat, rows16, rows16, dma((2,)), dma((2,)), *gather_sems, dma((2, NC)),
        ],
        compiler_params=pltpu.CompilerParams(collective_id=0, has_side_effects=True, vmem_limit_bytes=40 * 2**20),
        name="left_panel",
    )(momentum, gradient, factor)
    small = vmem((4, 8, RANK), F32)
    rfh, rfl, basis, update, ownf = pl.pallas_call(
        functools.partial(factor_kernel, n_cols=n_cols, scale=scale),
        out_shape=(
            shape((COLS, RANK), BF16), shape((COLS, RANK), BF16),
            shape((ROWS, RANK), F32), shape((ROWS, RANK), F32), shape((CH // 2, RANK), F32)),
        in_specs=[inside, inside, inside],
        out_specs=(hbm, hbm, inside, inside, inside),
        scratch_shapes=[
            flat, flat, vmem((2, 16, CA // 2, 128), F32), vmem((2, 16, CA, 128), F32),
            vmem((2, 9, CA, 128), F32), vmem((2, 2, 9, 2, CB, 128), F32), vmem((4, CB, 128), F32),
            vmem((RANK, RANK), F32), small, small, small, small, vmem((NC, 4, 8, RANK), F32),
            vmem((RANK, RANK), F32), vmem((COLS, RANK), BF16), vmem((COLS, RANK), BF16),
            vmem((8, RANK), F32), vmem((NC, 8, RANK), F32),
            dma((7,)), *gather_sems, dma((4, 16)), dma((2, 9)), dma((2, 2, 9)), dma((4,)),
            dma((5, NC)), dma((NC,)), dma((2,)),
        ],
        compiler_params=pltpu.CompilerParams(collective_id=1, has_side_effects=True, vmem_limit_bytes=48 * 2**20),
        name="right_factor",
    )(panel.reshape(ROWS, RANK), thi, tlo)
    whole = pl.BlockSpec((ROWS, RANK), lambda b: (0, 0))
    across = pl.BlockSpec((ROWS, BLK), lambda b: (0, b))
    down = pl.BlockSpec((BLK, RANK), lambda b: (b, 0))
    chunk = pl.BlockSpec((CH // 2, RANK), lambda b: (0, 0))
    return pl.pallas_call(
        output_kernel,
        grid=(NBLK,),
        out_shape=(shape((ROWS, COLS), F32), shape((ROWS, COLS), BF16), shape((CH // 2, RANK), F32)),
        in_specs=[across, across, down, down, whole, whole, chunk],
        out_specs=(across, across, chunk),
        compiler_params=pltpu.CompilerParams(vmem_limit_bytes=24 * 2**20),
        name="outputs",
    )(momentum, gradient, rfh, rfl, basis, update, ownf)


def solution(mesh):
    placed = (P("row", "col"), P("row", "col"), P(("col", "row"), None))
    return jax.shard_map(shards, mesh=mesh, in_specs=placed, out_specs=placed, check_vma=False)
```

time: 888 us -> 180 us (0.20)
  waiting for transfers between devices: 759 us -> 0 us
  Pallas kernels: 0 us -> 176 us
  other arithmetic: 58.4 us -> 0 us
  matrix products: 22 us -> 0 us
  blocking collectives: 21 us -> 0 us
  between operations: 15.3 us -> 0.67 us
    psum x3 -> x0, waiting for transfers between devices: 613 us -> none  [the longest x1 281 us: shards(): right_factor = lax.psum(transposed_product(buffer, left_basis), 'row')]
    pallas_call x0 -> x3, Pallas kernels: none -> 176 us  [the longest x1 106 us: shards(): pl.pallas_call(functools.partial(factor_kernel, n_cols=n_cols, scale=scal...]
    all_gather x1 -> x0, waiting for transfers between devices: 144 us -> none  [shards(): lax.all_gather(factor, 'row', axis=0, tiled=True)]
    another operation x9 -> x0, other arithmetic: 54.5 us -> none  [the longest x6 34 us: unit_columns(): lower_factor = jnp.linalg.cholesky(gram_matrix)]
    psum x1 -> x0, blocking collectives: 21 us -> none  [shards(): squares = lax.psum(jnp.sum(right_factor * right_factor, axis=0), 'col')]
    dot_general x5 -> x0, matrix products: 20.7 us -> none  [the longest x1 4.92 us: shards(): jnp.dot(left_basis, right_factor.T, precision=HIGHEST, preferred_element_...]
  transfers between devices with their start and end apart: 4 -> 0, of which waited for: 4 -> 0; matrix products, arithmetic and copies ran while one was open for 0% -> 0% of each run, Pallas kernels for 0% -> 0%
where the time goes in v1:
time: 180 us
  Pallas kernels  176 us (98%)
  local copies, waits for them, and re-layouts  3.43 us (2%)
    pallas_call x1, Pallas kernels, shards(): pl.pallas_call(functools.partial(factor_kernel, n_cols=n_cols, scale=scal...  106 us
    pallas_call x1, Pallas kernels, shards(): pl.pallas_call(panel_kernel, out_shape=(shape((NC, ROWS // NC, RANK), F32...  62.1 us
    pallas_call x1, Pallas kernels, shards(): pl.pallas_call(output_kernel, grid=(NBLK,), out_shape=(shape((ROWS, COLS)...  7.62 us

profile of v1, /device:TPU:1, one launch (start us, length us, event | category | flops | bytes accessed | tf_op | source)
XLA Modules:
  0.0 180.2 jit_solution(17228034531756368280)
XLA Ops:
  0.6 0.0 copy-start
  0.6 1.4 copy-done
  2.1 0.0 copy-start.2
  2.1 1.2 copy-done.2
  3.2 0.0 copy-start.4
  3.2 0.8 copy-done.4
  4.1 0.0 copy-start.1
  4.1 0.0 copy-start.3
  4.1 62.1 %left_panel.1 = (f32[8,16,256]{2,1,0:T(8,128)S(1)}, bf16[3328,128]{1,0:T(8,128)(2,1)S(1)}, bf16[3328,128]{1,0:T(8,128)(2,1)S(1)}) custom-call(f32[128,3328]{1,0:T(8,128)S(1)} %copy-done, bf16[128,3328]{1,0:T(8,128)(2,1)S(1)} %copy-done.2, f32[52,256]{1,0:T(8,128)S(1)} %copy-done.4), custom_call_target="tpu_custom_call" | custom-call | tf_op jit(solution)/shard_map/left_panel/pallas_call | solution.py:511
  66.2 106.4 %right_factor.1 = (bf16[3328,256]{1,0:T(8,128)(2,1)S(1)}, bf16[3328,256]{1,0:T(8,128)(2,1)S(1)}, f32[128,256]{1,0:T(8,128)S(1)}, f32[128,256]{1,0:T(8,128)S(1)}, f32[52,256]{1,0:T(8,128)S(1)}) custom-call(f32[128,256]{1,0:T(8,128)S(1)} %bitcast.1, bf16[3328,128]{1,0:T(8,128)(2,1)S(1)} %get-tuple-element.12.thi, bf16[3328,128]{1,0:T(8,128)(2,1)S(1)} %get-tuple-element.13.tlo), custom_call_target="tpu_custom_call" | custom-call | tf_op jit(solution)/shard_map/right_factor/pallas_call | solution.py:524
  172.5 0.0 copy-done.1
  172.5 0.0 copy-done.3
  172.5 7.6 %outputs.1 = (f32[128,3328]{1,0:T(8,128)}, bf16[128,3328]{1,0:T(8,128)(2,1)}, f32[52,256]{1,0:T(8,128)}) custom-call(f32[128,3328]{1,0:T(8,128)S(1)} %copy-done.1, bf16[128,3328]{1,0:T(8,128)(2,1)S(1)} %copy-done.3, bf16[3328,256]{1,0:T(8,128)(2,1)S(1)} %get-tuple-element.14.rfh, bf16[3328,256]{1,0:T(8,128)(2,1)S(1)} %get-tuple-element.15.rfl, ...), custom_call_target="tpu_custom_call" | custom-call | tf_op jit(solution)/shard_map/outputs/pallas_call | solution.py:547
Async XLA Ops:
  0.6 1.5 copy-start
  2.1 1.2 copy-start.2
  3.2 0.8 copy-start.4
  4.1 168.5 %copy-start.1 = (f32[128,3328]{1,0:T(8,128)S(1)}, f32[128,3328]{1,0:T(8,128)}, u32[]{:S(2)}) copy-start(f32[128,3328]{1,0:T(8,128)} %mom.3) | copy-start | bytes 5111812
  4.1 168.5 %copy-start.3 = (bf16[128,3328]{1,0:T(8,128)(2,1)S(1)}, bf16[128,3328]{1,0:T(8,128)(2,1)}, u32[]{:S(2)}) copy-start(bf16[128,3328]{1,0:T(8,128)(2,1)} %grad.3) | copy-start | bytes 2555908

commit v2 on v1

v2 whole, which is shorter than its diff:
```python
import functools
import math

import jax
import jax.numpy as jnp
from jax import lax
from jax.experimental import pallas as pl
from jax.experimental.pallas import tpu as pltpu
from jax.sharding import PartitionSpec as P

HIGHEST = lax.Precision.HIGHEST
MOMENTUM_KEEP = 0.8
STEP_SIZE = 0.3
EPSILON = 1e-06
F32 = jnp.float32
BF16 = jnp.bfloat16

NX, NZ = 4, 16
NC = 8
CH = 104
CA = 64
CB = CH - CA
ROWS, COLS, RANK = 128, 3328, 256
BLK = 256
NBLK = COLS // BLK
NB = 32


def split(value):
    high = value.astype(BF16)
    return high, (value - high.astype(F32)).astype(BF16)


def dot(a, b, dims=((1,), (0,))):
    return lax.dot_general(a, b, (dims, ((), ())), preferred_element_type=F32)


def dot3(a, b, dims=((1,), (0,))):
    return dot(a[0], b[0], dims) + (dot(a[0], b[1], dims) + dot(a[1], b[0], dims))


def dot6(a, b, dims=((1,), (0,))):
    return lax.dot_general(a, b, (dims, ((), ())), precision=HIGHEST, preferred_element_type=F32)


class Links:
    def __init__(self, ssem, rsem):
        self.ssem, self.rsem = ssem, rsem
        self.r, self.c = lax.axis_index("row"), lax.axis_index("col")
        self.x, self.z = self.r // NZ, self.r % NZ

        x, z, c = self.x, self.z, self.c
        self.xs = {d: {"row": lax.rem(x + d, NX) * NZ + z, "col": c} for d in (1, 2, 3)}
        self.zs = {d: {"row": x * NZ + lax.rem(z + d, NZ), "col": c} for d in (1, 4, 8, 12, 15)}
        self.qs = {d: {"row": x * NZ + (z // 4) * 4 + lax.rem(z + d, 4), "col": c} for d in (1, 2, 3)}
        self.cs = {d: {"row": self.r, "col": lax.rem(c + d, NC)} for d in range(1, NC)}

    def copy(self, src, dst, recv, device, slot=0):
        return pltpu.make_async_remote_copy(
            src_ref=src, dst_ref=dst, send_sem=self.ssem.at[slot], recv_sem=recv,
            device_id=device, device_id_type=pl.DeviceIdType.MESH)

    def send(self, src, dst, recv, device, slot):
        self.copy(src, dst, recv, device, slot).start()

    def recv(self, dst, sem):
        self.copy(dst, dst, sem, self.xs[1]).wait_recv()

    def sent(self, ref, slot):
        self.copy(ref, ref, self.rsem, self.xs[1], slot).wait_send()

    def greet(self, peers):
        barrier = pltpu.get_barrier_semaphore()
        for peer in peers:
            pl.semaphore_signal(barrier, inc=1, device_id=peer, device_id_type=pl.DeviceIdType.MESH)
        return lambda: pl.semaphore_wait(barrier, len(peers))


def block(b):
    return pl.ds(pl.multiple_of(b * BLK, BLK), BLK)


def split_rows(ref, b):
    parts = [split(ref[pl.ds(2 * BLK * b + h, BLK, stride=2), :]) for h in (0, 1)]
    return tuple(jnp.concatenate(p, axis=1) for p in zip(*parts))


def gather(t, buf, natural, sems, work):
    agaz, agax, agbx, agbz = sems
    xs, send, recv = t.xs, t.send, t.recv
    right, left = t.zs[1], t.zs[15]
    half = CA // 2

    def one(k):
        return buf.at[0, k, pl.ds(0, CA)]

    def two(i, k, n, lo=0, size=CA):
        return buf.at[i, pl.ds(k, n), pl.ds(lo, size)]

    def group(g, k):
        return buf.at[pl.ds(2 * g, 2), k, pl.ds(CA, CB)]

    def side(k, n, s):
        send(two(0, k, n), two(1, k, n), agax.at[0, s], xs[1], 0)
        send(two(0, k, n), two(3, k, n), agax.at[1, s], xs[3], 0)

    def forward(k, n, s):
        recv(two(1, k, n), agax.at[0, s])
        send(two(1, k, n, 0, half), two(2, k, n, 0, half), agax.at[2, s], xs[1], 0)
        recv(two(3, k, n), agax.at[1, s])
        send(two(3, k, n, half, half), two(2, k, n, half, half), agax.at[3, s], xs[3], 0)

    def finish(k, n, s):
        recv(two(2, k, n, 0, half), agax.at[2, s])
        recv(two(2, k, n, half, half), agax.at[3, s])

    for d in (1, 2, 3):
        send(buf.at[0, 0, pl.ds(CA, CB)], buf.at[d, 0, pl.ds(CA, CB)], agbx.at[d], xs[d], 0)
    send(one(0), one(1), agaz.at[0, 1], right, 0)
    send(one(0), one(2), agaz.at[1, 1], left, 0)
    side(0, 1, 0)
    for d in (1, 2, 3):
        recv(buf.at[d, 0, pl.ds(CA, CB)], agbx.at[d])
    for g in (0, 1):
        send(group(g, 0), group(g, 1), agbz.at[0, g, 1], right, 0)
        send(group(g, 0), group(g, 2), agbz.at[1, g, 1], left, 0)
    forward(0, 1, 0)

    def step(s, carry):
        kr, kl = 2 * s - 1, 2 * s
        recv(one(kr), agaz.at[0, s])
        send(one(kr), one(kr + 2), agaz.at[0, s + 1], right, 0)
        recv(one(kl), agaz.at[1, s])

        @pl.when(s < 7)
        def _():
            send(one(kl), one(kl + 2), agaz.at[1, s + 1], left, 0)

        side(kr, 2, s)
        for g in (0, 1):
            recv(group(g, kl), agbz.at[1, g, s])
            send(group(g, kl), group(g, jnp.minimum(kl + 2, 15)), agbz.at[1, g, s + 1], left, 0)
            recv(group(g, kr), agbz.at[0, g, s])

            @pl.when(s < 7)
            def _():
                send(group(g, kr), group(g, kr + 2), agbz.at[0, g, s + 1], right, 0)

        @pl.when(s > 1)
        def _():
            forward(kr - 2, 2, s - 1)

        work(s)
        return carry

    lax.fori_loop(1, 8, step, 0)
    recv(one(15), agaz.at[0, 8])
    side(15, 1, 8)
    forward(13, 2, 7)
    for g in (0, 1):
        recv(group(g, 15), agbz.at[1, g, 8])
    forward(15, 1, 8)
    finish(0, 1, 0)

    def last(s, carry):
        finish(2 * s - 1, 2, s)
        return carry

    lax.fori_loop(1, 8, last, 0)
    finish(15, 1, 8)
    t.sent(buf.reshape(NX * NZ * CH, 128).at[pl.ds(0, 6552)], 0)

    def place(n, carry):
        s = lax.rem(t.z - n + 2 * NZ, NZ)
        k = jnp.where(s == 0, 0, jnp.where(s > 8, 2 * (NZ - s), 2 * s - 1))
        for i in range(NX):
            row = lax.rem(t.x - i + NX, NX) * NZ + n
            natural[pl.ds(pl.multiple_of(CH * row, 8), CH), :] = buf[i, k]
        return carry

    lax.fori_loop(0, NZ, place, 0)


def panel_kernel(mom, grad, fac, panel, thi, tlo, momv, gradv, bhi, blo, gat, gat2, ppart, precv,
                 lsem, ssem, agaz, agax, agbx, agbz, psem):
    t = Links(ssem, agbx.at[0])
    c, cs, send, recv, sent = t.c, t.cs, t.send, t.recv, t.sent
    loads = (pltpu.make_async_copy(mom, momv, lsem.at[0]), pltpu.make_async_copy(grad, gradv, lsem.at[1]))
    for load in loads:
        load.start()
    greeted = t.greet([*t.xs.values(), *cs.values(), t.zs[1], t.zs[15]])

    gat.at[0, 0][pl.ds(0, CH // 2, stride=2), :] = fac[:, :128]
    gat.at[0, 0][pl.ds(1, CH // 2, stride=2), :] = fac[:, 128:]
    greeted()

    def prepare(b):
        at = block(b)
        value = momv[:, at] + gradv[:, at].astype(F32)
        high, low = split(value)
        bhi[:, at], blo[:, at] = high, low
        high, low = split(value.T)
        thi[at, :], tlo[at, :] = high, low

    def prepare_step(s):
        @pl.when(s == 1)
        def _():
            for load in loads:
                load.wait()

        prepare(2 * s - 2)

        @pl.when(s < 7)
        def _():
            prepare(2 * s - 1)

    gather(t, gat, gat2, (agaz, agax, agbx, agbz), prepare_step)

    def panel_step(b, total):
        at = block(b)
        return total + dot3((bhi[:, at], blo[:, at]), split_rows(gat2, b))

    total = lax.fori_loop(0, NBLK, panel_step, jnp.zeros((ROWS, RANK), F32))
    ppart[...] = total.reshape(NC, ROWS // NC, RANK)
    for d in range(1, NC):
        send(ppart.at[cs[d]["col"]], precv.at[d], psem.at[0, d], cs[d], 1)
    mine = ppart[c]
    for d in range(1, NC):
        recv(precv.at[d], psem.at[0, d])
        mine = mine + precv[d]
    panel[c] = mine
    for d in range(1, NC):
        send(panel.at[c], panel.at[c], psem.at[1, d], cs[d], 1)
    for d in range(1, NC):
        recv(panel.at[lax.rem(c - d + NC, NC)], psem.at[1, d])
    sent(gat2.at[pl.ds(0, 14 * 32)], 1)


def factor_kernel(panel, thi, tlo, rfh, rfl, basis, update, ownf,
                  term, part, red, red2, xh, xf, za, zb, xb, gram, g0, g1, g2, g3, g4, aw, rfhv, rflv, sq, sqr,
                  ssem, agaz, agax, agbx, agbz, rsx, rsza, rszb, rsxb, gsem, qsem, osem, *, n_cols, scale):
    t = Links(ssem, agbx.at[0])
    r, c, x, z = t.r, t.c, t.x, t.z
    xs, zs, qs, cs, send, recv, sent = t.xs, t.zs, t.qs, t.cs, t.send, t.recv, t.sent
    greeted = t.greet([*xs.values(), *zs.values(), *qs.values(), *cs.values()])

    left = panel[...]
    gram[...] = dot6(left.T, left)
    greeted()

    def gram_rows(xi):
        return pl.ds(pl.multiple_of(32 * c + 8 * xi, 8), 8)

    for d in (1, 2, 3):
        send(gram.at[gram_rows(lax.rem(x + d, NX))], g0.at[d], gsem.at[0, d], xs[d], 2)

    def gram_0():
        total = gram[gram_rows(x), :]
        for d in (1, 2, 3):
            recv(g0.at[d], gsem.at[0, d])
            total = total + g0[d]
        g1[0] = total
        for d in (1, 2, 3):
            send(g1.at[0], g1.at[d], gsem.at[1, d], qs[d], 2)

    def gram_1():
        total = g1[0]
        for d in (1, 2, 3):
            recv(g1.at[d], gsem.at[1, d])
            total = total + g1[d]
        g2[0] = total
        for d in (1, 2, 3):
            send(g2.at[0], g2.at[d], gsem.at[2, d], zs[4 * d], 2)

    def gram_2():
        total = g2[0]
        for d in (1, 2, 3):
            recv(g2.at[d], gsem.at[2, d])
            total = total + g2[d]
        g3[x] = total
        for d in (1, 2, 3):
            send(g3.at[x], g3.at[x], gsem.at[3, d], xs[d], 2)

    def gram_3():
        for d in (1, 2, 3):
            recv(g3.at[lax.rem(x - d + NX, NX)], gsem.at[3, d])
        g4[c] = g3[...]
        for d in range(1, NC):
            send(g4.at[c], g4.at[c], gsem.at[4, d], cs[d], 3)

    def gram_4():
        for d in range(1, NC):
            recv(g4.at[lax.rem(c - d + NC, NC)], gsem.at[4, d])
        aw[...] = g4[...].reshape(RANK, RANK)
        sent(gram.at[pl.ds(0, 96)], 2)
        sent(g4.at[pl.ds(0, NC - 1)], 3)

    sub = lax.broadcasted_iota(jnp.int32, (NB, 128), 0)
    lane = lax.broadcasted_iota(jnp.int32, (NB, 128), 1)
    sub_w = lax.broadcasted_iota(jnp.int32, (NB, RANK), 0)
    lane_w = lax.broadcasted_iota(jnp.int32, (NB, RANK), 1)
    i_all = lax.broadcasted_iota(jnp.int32, (RANK, RANK), 0)
    j_all = lax.broadcasted_iota(jnp.int32, (RANK, RANK), 1)

    def factor_block(k):
        first = pl.multiple_of(NB * k, NB)
        rows = aw[pl.ds(first, NB), :]
        near = jnp.where(k < 4, rows[:, :128], rows[:, 128:])
        near = pltpu.roll(near, lax.rem(128 - NB * lax.rem(k, 4), 128), 1)
        e = jnp.where(lane < NB, near, jnp.where(lane - NB == sub, 1.0, 0.0))
        for j in range(0, NB, 4):
            cols = [jnp.broadcast_to(e[:, j + i:j + i + 1], (NB, 128)) for i in range(4)]
            pivots = [e[j + i:j + i + 1, :] for i in range(4)]
            for i in range(4):
                at = slice(j + i, j + i + 1)
                ratio = jnp.where(sub > j + i, cols[i] * (1.0 / cols[i][at, :]), 0.0)
                for m in range(i + 1, 4):
                    cols[m] = cols[m] - ratio * cols[m][at, :]
                    pivots[m] = pivots[m] - ratio[j + m:j + m + 1, :] * pivots[i]
                e = e - ratio * pivots[i]
        diagonal = jnp.sum(jnp.where(lane == sub, e, 0.0), axis=1, keepdims=True)
        inverse = (e * (1.0 / jnp.sqrt(diagonal)))[:, NB:2 * NB]
        here = (lane_w >= first) & (lane_w < first + NB)
        rows = jnp.where(here, jnp.where(lane_w - first == sub_w, 1.0, 0.0), rows)
        rows = dot6(inverse, rows)
        below = jnp.where(lane_w >= first + NB, rows, 0.0)
        done = (i_all >= first + NB) & (j_all >= first) & (j_all < first + NB)
        aw[...] = jnp.where(done, 0.0, aw[...]) - dot6(below.T, rows)
        aw[pl.ds(first, NB), :] = rows

    lp = split(left)

    def term_step(b, carry):
        h = dot3((thi[block(b), :], tlo[block(b), :]), lp)
        term[pl.ds(2 * BLK * b, BLK, stride=2), :] = h[:, :128]
        term[pl.ds(2 * BLK * b + 1, BLK, stride=2), :] = h[:, 128:]
        pl.when(b == 6)(gram_0)
        return carry

    lax.fori_loop(0, NBLK, term_step, 0)
    gram_1()

    def place(k, carry):
        n = lax.rem(jnp.where(lax.rem(k, 2) == 0, z + 8 - k // 2, jnp.where(k == 15, z, z + 9 + k // 2)), NZ)
        for i in range(NX):
            row = lax.rem(x + i, NX) * NZ + n
            part[i, k] = term[pl.ds(pl.multiple_of(CH * row, 8), CH), :]
        return carry

    lax.fori_loop(0, NZ, place, 0)

    half = CA // 2

    def pair(i, s, lo=0, size=CA):
        return part.at[i, pl.ds(2 * s, 2), pl.ds(lo, size)]

    def send_half(s):
        send(pair(2, s, 0, half), xh.at[0, s], rsx.at[0, s], xs[1], 4)
        send(pair(2, s, half, half), xh.at[1, s], rsx.at[1, s], xs[3], 4)

    def send_full(s):
        two = pl.ds(2 * s, 2)
        recv(xh.at[0, s], rsx.at[0, s])
        part[1, two, :half, :] += xh[0, s]
        send(pair(1, s), xf.at[0, s], rsx.at[2, s], xs[1], 4)
        recv(xh.at[1, s], rsx.at[1, s])
        part[3, two, half:CA, :] += xh[1, s]
        send(pair(3, s), xf.at[1, s], rsx.at[3, s], xs[3], 4)

    def take_full(s):
        two = pl.ds(2 * s, 2)
        recv(xf.at[0, s], rsx.at[2, s])
        recv(xf.at[1, s], rsx.at[3, s])
        part[0, two, :CA, :] += xf[0, s] + xf[1, s]

    send_half(0)
    send_half(1)
    send_full(0)

    def reduce_step(s, carry):
        @pl.when(s < 6)
        def _():
            send_half(s + 2)

        for i, g in enumerate((1, 0)):
            rows = pl.ds(2 * g, 2)
            kl, kr = jnp.maximum(2 * s - 1, 0), 2 * s + 2

            @pl.when(s > 0)
            def _():
                recv(zb.at[1, i, s], rszb.at[1, i, s])
                part[rows, kl, CA:, :] += zb[1, i, s]

            send(part.at[rows, kl, pl.ds(CA, CB)], zb.at[1, i, s + 1], rszb.at[1, i, s + 1], zs[15], 4)

            @pl.when(s < 7)
            def _():
                @pl.when(s > 0)
                def _():
                    recv(zb.at[0, i, s], rszb.at[0, i, s])
                    part[rows, kr, CA:, :] += zb[0, i, s]

                send(part.at[rows, kr, pl.ds(CA, CB)], zb.at[0, i, s + 1], rszb.at[0, i, s + 1], zs[1], 4)

        @pl.when(s < 7)
        def _():
            send_full(s + 1)

        take_full(s)

        @pl.when(s > 0)
        def _():
            recv(za.at[0, s], rsza.at[0, s])
            part[0, 2 * s, :CA, :] += za[0, s]

        send(part.at[0, 2 * s, pl.ds(0, CA)], za.at[0, s + 1], rsza.at[0, s + 1], zs[1], 4)

        @pl.when(s < 7)
        def _():
            @pl.when(s > 0)
            def _():
                recv(za.at[1, s], rsza.at[1, s])
                part[0, 2 * s + 1, :CA, :] += za[1, s]

            send(part.at[0, 2 * s + 1, pl.ds(0, CA)], za.at[1, s + 1], rsza.at[1, s + 1], zs[15], 4)

        for when, stage in enumerate((gram_2, gram_3, gram_4)):
            pl.when(s == when)(stage)

        @pl.when(s > 2)
        def _():
            factor_block(s - 3)

        return carry

    lax.fori_loop(0, 8, reduce_step, 0)
    for i, g in enumerate((1, 0)):
        recv(zb.at[1, i, 8], rszb.at[1, i, 8])
        recv(zb.at[0, i, 7], rszb.at[0, i, 7])
        part[2 * g:2 * g + 2, 15, CA:, :] += zb[1, i, 8] + zb[0, i, 7]
    for d in (1, 2, 3):
        send(part.at[d, 15, pl.ds(CA, CB)], xb.at[d], rsxb.at[d], xs[d], 4)
    recv(za.at[0, 8], rsza.at[0, 8])
    recv(za.at[1, 7], rsza.at[1, 7])
    red[0, 0, :CA, :] = part[0, 15, :CA, :] + (za[0, 8] + za[1, 7])
    total = part[0, 15, CA:, :]
    for d in (1, 2, 3):
        recv(xb.at[d], rsxb.at[d])
        total = total + xb[d]
    red[0, 0, CA:, :] = total
    sent(term.at[pl.ds(0, 6552)], 4)

    def factor_rest(s):
        @pl.when(s < 4)
        def _():
            factor_block(s + 4)

    gather(t, red, red2, (agaz, agax, agbx, agbz), factor_rest)

    inverse = jnp.where(i_all >= j_all, aw[...], 0.0)
    nt = ((1,), (1,))
    inv = split(inverse)

    def right_step(b, squares):
        rf = dot3(split_rows(red2, b), inv, nt)
        rfhv[block(b), :], rflv[block(b), :] = split(rf)
        return squares + jnp.sum((rf * rf).reshape(BLK // 8, 8, RANK), axis=0)

    squares = lax.fori_loop(0, NBLK, right_step, jnp.zeros((8, RANK), F32))
    stores = (pltpu.make_async_copy(rfhv, rfh, osem.at[0]), pltpu.make_async_copy(rflv, rfl, osem.at[1]))
    for store in stores:
        store.start()
    sq[...] = squares
    for d in range(1, NC):
        send(sq, sqr.at[d], qsem.at[d], cs[d], 6)
    left_basis = dot6(left, inverse, nt)
    halves = [red.at[0, 0][pl.ds(h, CH // 2, stride=2), :] for h in (0, 1)]
    own_rf = dot6(jnp.concatenate(halves, axis=1), inverse, nt)
    for d in range(1, NC):
        recv(sqr.at[d], qsem.at[d])
        squares = squares + sqr[d]
    rms = jnp.sqrt(jnp.sum(squares, axis=0, keepdims=True) * (1.0 / n_cols) + EPSILON)
    ownf[...] = own_rf / rms
    basis[...] = left_basis * -(1.0 - MOMENTUM_KEEP)
    update[...] = left_basis * (-scale / rms)
    sent(gram.at[pl.ds(0, 8 * (NC - 1))], 6)
    for store in stores:
        store.wait()


def output_kernel(mom, grad, rfh, rfl, basis, update, ownf, momo, wupd, faco):
    nt = ((1,), (1,))
    high, low = split(update[...])
    rows = jnp.concatenate([basis[...].astype(BF16), high, low], axis=0)
    product = dot(rows, rfh[...], nt)
    momo[...] = mom[...] + grad[...].astype(F32) + product[:ROWS]
    wupd[...] = (product[ROWS:2 * ROWS] + (product[2 * ROWS:] + dot(high, rfl[...], nt))).astype(BF16)

    @pl.when(pl.program_id(0) == 0)
    def _():
        faco[...] = ownf[...]


def shards(momentum, gradient, factor):
    rows = momentum.shape[0] * lax.axis_size("row")
    n_cols = momentum.shape[1] * lax.axis_size("col")
    scale = STEP_SIZE * math.sqrt(rows / factor.shape[1])
    dma, vmem, hbm = pltpu.SemaphoreType.DMA, pltpu.VMEM, pl.BlockSpec(memory_space=pl.ANY)
    inside = pl.BlockSpec(memory_space=pltpu.VMEM)
    shape = jax.ShapeDtypeStruct
    flat, natural = vmem((NX, NZ, CH, 128), F32), vmem((NX * NZ * CH, 128), F32)
    gather_sems = [dma((2, 9)), dma((4, 9)), dma((4,)), dma((2, 2, 9))]
    rows16 = vmem((NC, ROWS // NC, RANK), F32)
    panel, thi, tlo = pl.pallas_call(
        panel_kernel,
        out_shape=(shape((NC, ROWS // NC, RANK), F32), shape((COLS, ROWS), BF16), shape((COLS, ROWS), BF16)),
        in_specs=[hbm, hbm, inside],
        out_specs=(inside, inside, inside),
        scratch_shapes=[
            vmem((ROWS, COLS), F32), vmem((ROWS, COLS), BF16), vmem((ROWS, COLS), BF16), vmem((ROWS, COLS), BF16),
            flat, natural, rows16, rows16, dma((2,)), dma((2,)), *gather_sems, dma((2, NC)),
        ],
        compiler_params=pltpu.CompilerParams(collective_id=0, has_side_effects=True, vmem_limit_bytes=60 * 2**20),
        name="left_panel",
    )(momentum, gradient, factor)
    small = vmem((4, 8, RANK), F32)
    rfh, rfl, basis, update, ownf = pl.pallas_call(
        functools.partial(factor_kernel, n_cols=n_cols, scale=scale),
        out_shape=(
            shape((COLS, RANK), BF16), shape((COLS, RANK), BF16),
            shape((ROWS, RANK), F32), shape((ROWS, RANK), F32), shape((CH // 2, RANK), F32)),
        in_specs=[inside, inside, inside],
        out_specs=(hbm, hbm, inside, inside, inside),
        scratch_shapes=[
            natural, flat, flat, natural, vmem((2, 8, 2, CA // 2, 128), F32), vmem((2, 8, 2, CA, 128), F32),
            vmem((2, 9, CA, 128), F32), vmem((2, 2, 9, 2, CB, 128), F32), vmem((4, CB, 128), F32),
            vmem((RANK, RANK), F32), small, small, small, small, vmem((NC, 4, 8, RANK), F32),
            vmem((RANK, RANK), F32), vmem((COLS, RANK), BF16), vmem((COLS, RANK), BF16),
            vmem((8, RANK), F32), vmem((NC, 8, RANK), F32),
            dma((7,)), *gather_sems, dma((4, 8)), dma((2, 9)), dma((2, 2, 9)), dma((4,)),
            dma((5, NC)), dma((NC,)), dma((2,)),
        ],
        compiler_params=pltpu.CompilerParams(collective_id=1, has_side_effects=True, vmem_limit_bytes=60 * 2**20),
        name="right_factor",
    )(panel.reshape(ROWS, RANK), thi, tlo)
    whole = pl.BlockSpec((ROWS, RANK), lambda b: (0, 0))
    across = pl.BlockSpec((ROWS, BLK), lambda b: (0, b))
    down = pl.BlockSpec((BLK, RANK), lambda b: (b, 0))
    chunk = pl.BlockSpec((CH // 2, RANK), lambda b: (0, 0))
    return pl.pallas_call(
        output_kernel,
        grid=(NBLK,),
        out_shape=(shape((ROWS, COLS), F32), shape((ROWS, COLS), BF16), shape((CH // 2, RANK), F32)),
        in_specs=[across, across, down, down, whole, whole, chunk],
        out_specs=(across, across, chunk),
        compiler_params=pltpu.CompilerParams(vmem_limit_bytes=60 * 2**20),
        name="outputs",
    )(momentum, gradient, rfh, rfl, basis, update, ownf)


def solution(mesh):
    placed = (P("row", "col"), P("row", "col"), P(("col", "row"), None))
    return jax.shard_map(shards, mesh=mesh, in_specs=placed, out_specs=placed, check_vma=False)
```

time: 180 us -> 179 us (level)
  local copies, waits for them, and re-layouts: 3.43 us -> 0 us
  Pallas kernels: 176 us -> 178 us
    unnamed x10 -> x0, local copies, waits for them, and re-layouts: 3.43 us -> none
    pallas_call x1, Pallas kernels: 7.62 us -> 10.9 us  [shards(): pl.pallas_call(output_kernel, grid=(NBLK,), out_shape=(shape((ROWS, COLS)...]
    pallas_call x1, Pallas kernels: 106 us -> 104 us  [shards(): pl.pallas_call(functools.partial(factor_kernel, n_cols=n_cols, scale=scal...]
where the time goes in v2:
time: 179 us
  Pallas kernels  178 us (99%)
    pallas_call x1, Pallas kernels, shards(): pl.pallas_call(functools.partial(factor_kernel, n_cols=n_cols, scale=scal...  104 us
    pallas_call x1, Pallas kernels, shards(): pl.pallas_call(panel_kernel, out_shape=(shape((NC, ROWS // NC, RANK), F32...  63.7 us
    pallas_call x1, Pallas kernels, shards(): pl.pallas_call(output_kernel, grid=(NBLK,), out_shape=(shape((ROWS, COLS)...  10.9 us

profile of v2, /device:TPU:1, one launch (start us, length us, event | category | flops | bytes accessed | tf_op | source)
XLA Modules:
  0.0 178.8 jit_solution(16204078225838488906)
XLA Ops:
  0.6 63.7 %left_panel.1 = (f32[8,16,256]{2,1,0:T(8,128)}, bf16[3328,128]{1,0:T(8,128)(2,1)}, bf16[3328,128]{1,0:T(8,128)(2,1)}) custom-call(f32[128,3328]{1,0:T(8,128)} %mom.3, bf16[128,3328]{1,0:T(8,128)(2,1)} %grad.3, f32[52,256]{1,0:T(8,128)} %fac.1), custom_call_target="tpu_custom_call" | custom-call | tf_op jit(solution)/shard_map/left_panel/pallas_call | solution.py:514
  64.3 103.6 %right_factor.1 = (bf16[3328,256]{1,0:T(8,128)(2,1)}, bf16[3328,256]{1,0:T(8,128)(2,1)}, f32[128,256]{1,0:T(8,128)}, f32[128,256]{1,0:T(8,128)}, f32[52,256]{1,0:T(8,128)}) custom-call(f32[128,256]{1,0:T(8,128)} %bitcast.1, bf16[3328,128]{1,0:T(8,128)(2,1)} %get-tuple-element.12.thi, bf16[3328,128]{1,0:T(8,128)(2,1)} %get-tuple-element.13.tlo), custom_call_target="tpu_custom_call" | custom-call | tf_op jit(solution)/shard_map/right_factor/pallas_call | solution.py:527
  167.9 10.9 %outputs.1 = (f32[128,3328]{1,0:T(8,128)}, bf16[128,3328]{1,0:T(8,128)(2,1)}, f32[52,256]{1,0:T(8,128)}) custom-call(f32[128,3328]{1,0:T(8,128)} %mom.3, bf16[128,3328]{1,0:T(8,128)(2,1)} %grad.3, bf16[3328,256]{1,0:T(8,128)(2,1)} %get-tuple-element.14.rfh, bf16[3328,256]{1,0:T(8,128)(2,1)} %get-tuple-element.15.rfl, f32[128,256]{1,0:T(8,128)} %get-tuple-element.16.basis, ...), custom_call_target="tpu_custom_call" | custom-call | tf_op jit(solution)/shard_map/outputs/pallas_call | solution.py:550

commit v3 on v2

--- a/solution.py
+++ b/solution.py
@@ -23,6 +23,7 @@
 ROWS, COLS, RANK = 128, 3328, 256
 BLK = 256
 NBLK = COLS // BLK
+HALF = COLS // 2
 NB = 32
 
 
@@ -51,7 +52,7 @@
 
         x, z, c = self.x, self.z, self.c
         self.xs = {d: {"row": lax.rem(x + d, NX) * NZ + z, "col": c} for d in (1, 2, 3)}
-        self.zs = {d: {"row": x * NZ + lax.rem(z + d, NZ), "col": c} for d in (1, 4, 8, 12, 15)}
+        self.zs = {d: {"row": x * NZ + lax.rem(z + d, NZ), "col": c} for d in (1, 4, 5, 8, 11, 12, 15)}
         self.qs = {d: {"row": x * NZ + (z // 4) * 4 + lax.rem(z + d, 4), "col": c} for d in (1, 2, 3)}
         self.cs = {d: {"row": self.r, "col": lax.rem(c + d, NC)} for d in range(1, NC)}
 
@@ -71,6 +72,7 @@
 
     def greet(self, peers):
         barrier = pltpu.get_barrier_semaphore()
+        peers = list(peers)
         for peer in peers:
             pl.semaphore_signal(barrier, inc=1, device_id=peer, device_id_type=pl.DeviceIdType.MESH)
         return lambda: pl.semaphore_wait(barrier, len(peers))
@@ -181,14 +183,12 @@
     lax.fori_loop(0, NZ, place, 0)
 
 
-def panel_kernel(mom, grad, fac, panel, thi, tlo, momv, gradv, bhi, blo, gat, gat2, ppart, precv,
-                 lsem, ssem, agaz, agax, agbx, agbz, psem):
-    t = Links(ssem, agbx.at[0])
-    c, cs, send, recv, sent = t.c, t.cs, t.send, t.recv, t.sent
+def gather_kernel(mom, grad, fac, gat2, bhi, blo, thi, tlo, momv, gradv, gat, lsem, ssem, *sems):
+    t = Links(ssem, sems[0].at[0, 0])
     loads = (pltpu.make_async_copy(mom, momv, lsem.at[0]), pltpu.make_async_copy(grad, gradv, lsem.at[1]))
     for load in loads:
         load.start()
-    greeted = t.greet([*t.xs.values(), *cs.values(), t.zs[1], t.zs[15]])
+    greeted = t.greet([*t.xs.values(), t.zs[1], t.zs[15]])
 
     gat.at[0, 0][pl.ds(0, CH // 2, stride=2), :] = fac[:, :128]
     gat.at[0, 0][pl.ds(1, CH // 2, stride=2), :] = fac[:, 128:]
@@ -214,7 +214,13 @@
         def _():
             prepare(2 * s - 1)
 
-    gather(t, gat, gat2, (agaz, agax, agbx, agbz), prepare_step)
+    gather(t, gat, gat2, sems, prepare_step)
+
+
+def panel_kernel(gat2, bhi, blo, panel, ppart, precv, ssem, psem):
+    t = Links(ssem, psem.at[0, 0])
+    c, cs, send, recv, sent = t.c, t.cs, t.send, t.recv, t.sent
+    greeted = t.greet(cs.values())
 
     def panel_step(b, total):
         at = block(b)
@@ -222,27 +228,28 @@
 
     total = lax.fori_loop(0, NBLK, panel_step, jnp.zeros((ROWS, RANK), F32))
     ppart[...] = total.reshape(NC, ROWS // NC, RANK)
+    greeted()
     for d in range(1, NC):
-        send(ppart.at[cs[d]["col"]], precv.at[d], psem.at[0, d], cs[d], 1)
+        send(ppart.at[cs[d]["col"]], precv.at[d], psem.at[0, d], cs[d], 0)
     mine = ppart[c]
     for d in range(1, NC):
         recv(precv.at[d], psem.at[0, d])
         mine = mine + precv[d]
     panel[c] = mine
     for d in range(1, NC):
-        send(panel.at[c], panel.at[c], psem.at[1, d], cs[d], 1)
+        send(panel.at[c], panel.at[c], psem.at[1, d], cs[d], 0)
     for d in range(1, NC):
         recv(panel.at[lax.rem(c - d + NC, NC)], psem.at[1, d])
-    sent(gat2.at[pl.ds(0, 14 * 32)], 1)
-
-
-def factor_kernel(panel, thi, tlo, rfh, rfl, basis, update, ownf,
-                  term, part, red, red2, xh, xf, za, zb, xb, gram, g0, g1, g2, g3, g4, aw, rfhv, rflv, sq, sqr,
-                  ssem, agaz, agax, agbx, agbz, rsx, rsza, rszb, rsxb, gsem, qsem, osem, *, n_cols, scale):
+    sent(gat2.at[pl.ds(0, 14 * 32)], 0)
+
+
+def factor_kernel(panel, thi, tlo, red2, lower, own,
+                  term, part, red, xh, xf, za, zb, xb, gram, g0, g1, g2, g3, g4, aw,
+                  ssem, agaz, agax, agbx, agbz, rsx, rsza, rszb, rsxb, gsem):
     t = Links(ssem, agbx.at[0])
     r, c, x, z = t.r, t.c, t.x, t.z
     xs, zs, qs, cs, send, recv, sent = t.xs, t.zs, t.qs, t.cs, t.send, t.recv, t.sent
-    greeted = t.greet([*xs.values(), *zs.values(), *qs.values(), *cs.values()])
+    greeted = t.greet([*xs.values(), *(zs[d] for d in (1, 4, 8, 12, 15)), *qs.values(), *cs.values()])
 
     left = panel[...]
     gram[...] = dot6(left.T, left)
@@ -456,8 +463,17 @@
             factor_block(s + 4)
 
     gather(t, red, red2, (agaz, agax, agbx, agbz), factor_rest)
-
-    inverse = jnp.where(i_all >= j_all, aw[...], 0.0)
+    lower[...] = jnp.where(i_all >= j_all, aw[...], 0.0)
+    own[...] = red[0, 0]
+
+
+def scale_kernel(panel, red2, lower, own, rfh, rfl, basis, update, ownf, rfhv, rflv, sq, sqr,
+                 ssem, qsem, osem, *, n_cols, scale):
+    t = Links(ssem, qsem.at[0])
+    cs, send, recv, sent = t.cs, t.send, t.recv, t.sent
+    greeted = t.greet(cs.values())
+
+    inverse = lower[...]
     nt = ((1,), (1,))
     inv = split(inverse)
 
@@ -471,10 +487,11 @@
     for store in stores:
         store.start()
     sq[...] = squares
+    greeted()
     for d in range(1, NC):
-        send(sq, sqr.at[d], qsem.at[d], cs[d], 6)
-    left_basis = dot6(left, inverse, nt)
-    halves = [red.at[0, 0][pl.ds(h, CH // 2, stride=2), :] for h in (0, 1)]
+        send(sq, sqr.at[d], qsem.at[d], cs[d], 0)
+    left_basis = dot6(panel[...], inverse, nt)
+    halves = [own[pl.ds(h, CH // 2, stride=2), :] for h in (0, 1)]
     own_rf = dot6(jnp.concatenate(halves, axis=1), inverse, nt)
     for d in range(1, NC):
         recv(sqr.at[d], qsem.at[d])
@@ -483,7 +500,7 @@
     ownf[...] = own_rf / rms
     basis[...] = left_basis * -(1.0 - MOMENTUM_KEEP)
     update[...] = left_basis * (-scale / rms)
-    sent(gram.at[pl.ds(0, 8 * (NC - 1))], 6)
+    sent(sqr.at[pl.ds(0, NC - 1)], 0)
     for store in stores:
         store.wait()
 
@@ -492,9 +509,11 @@
     nt = ((1,), (1,))
     high, low = split(update[...])
     rows = jnp.concatenate([basis[...].astype(BF16), high, low], axis=0)
-    product = dot(rows, rfh[...], nt)
-    momo[...] = mom[...] + grad[...].astype(F32) + product[:ROWS]
-    wupd[...] = (product[ROWS:2 * ROWS] + (product[2 * ROWS:] + dot(high, rfl[...], nt))).astype(BF16)
+    for first in range(0, HALF, BLK):
+        at = slice(first, min(first + BLK, HALF))
+        product = dot(rows, rfh[at, :], nt)
+        momo[:, at] = mom[:, at] + grad[:, at].astype(F32) + product[:ROWS]
+        wupd[:, at] = (product[ROWS:2 * ROWS] + (product[2 * ROWS:] + dot(high, rfl[at, :], nt))).astype(BF16)
 
     @pl.when(pl.program_id(0) == 0)
     def _():
@@ -510,46 +529,50 @@
     shape = jax.ShapeDtypeStruct
     flat, natural = vmem((NX, NZ, CH, 128), F32), vmem((NX * NZ * CH, 128), F32)
     gather_sems = [dma((2, 9)), dma((4, 9)), dma((4,)), dma((2, 2, 9))]
+
+    def call(body, name, collective, inputs, outputs, scratch):
+        return pl.pallas_call(
+            body, name=name, out_shape=tuple(o[0] for o in outputs), out_specs=tuple(o[1] for o in outputs),
+            in_specs=[i[1] for i in inputs], scratch_shapes=scratch,
+            compiler_params=pltpu.CompilerParams(
+                collective_id=collective, has_side_effects=True, vmem_limit_bytes=60 * 2**20),
+        )(*(i[0] for i in inputs))
+
+    narrow, tall = (shape((ROWS, COLS), BF16), inside), (shape((COLS, ROWS), BF16), inside)
+    gathered = (shape((NX * NZ * CH, 128), F32), inside)
+    square, chunk = (shape((RANK, RANK), F32), inside), (shape((CH, 128), F32), inside)
+    gat, bhi, blo, thi, tlo = call(
+        gather_kernel, "gather_factor", 0, [(momentum, hbm), (gradient, hbm), (factor, inside)],
+        [gathered, narrow, narrow, tall, tall],
+        [vmem((ROWS, COLS), F32), vmem((ROWS, COLS), BF16), flat, dma((2,)), dma((1,)), *gather_sems])
     rows16 = vmem((NC, ROWS // NC, RANK), F32)
-    panel, thi, tlo = pl.pallas_call(
-        panel_kernel,
-        out_shape=(shape((NC, ROWS // NC, RANK), F32), shape((COLS, ROWS), BF16), shape((COLS, ROWS), BF16)),
-        in_specs=[hbm, hbm, inside],
-        out_specs=(inside, inside, inside),
-        scratch_shapes=[
-            vmem((ROWS, COLS), F32), vmem((ROWS, COLS), BF16), vmem((ROWS, COLS), BF16), vmem((ROWS, COLS), BF16),
-            flat, natural, rows16, rows16, dma((2,)), dma((2,)), *gather_sems, dma((2, NC)),
-        ],
-        compiler_params=pltpu.CompilerParams(collective_id=0, has_side_effects=True, vmem_limit_bytes=60 * 2**20),
-        name="left_panel",
-    )(momentum, gradient, factor)
+    (panel,) = call(
+        panel_kernel, "left_panel", 1, [(gat, inside), (bhi, inside), (blo, inside)],
+        [(shape((NC, ROWS // NC, RANK), F32), inside)], [rows16, rows16, dma((1,)), dma((2, NC))])
+    panel = panel.reshape(ROWS, RANK)
     small = vmem((4, 8, RANK), F32)
-    rfh, rfl, basis, update, ownf = pl.pallas_call(
-        functools.partial(factor_kernel, n_cols=n_cols, scale=scale),
-        out_shape=(
-            shape((COLS, RANK), BF16), shape((COLS, RANK), BF16),
-            shape((ROWS, RANK), F32), shape((ROWS, RANK), F32), shape((CH // 2, RANK), F32)),
-        in_specs=[inside, inside, inside],
-        out_specs=(hbm, hbm, inside, inside, inside),
-        scratch_shapes=[
-            natural, flat, flat, natural, vmem((2, 8, 2, CA // 2, 128), F32), vmem((2, 8, 2, CA, 128), F32),
-            vmem((2, 9, CA, 128), F32), vmem((2, 2, 9, 2, CB, 128), F32), vmem((4, CB, 128), F32),
-            vmem((RANK, RANK), F32), small, small, small, small, vmem((NC, 4, 8, RANK), F32),
-            vmem((RANK, RANK), F32), vmem((COLS, RANK), BF16), vmem((COLS, RANK), BF16),
-            vmem((8, RANK), F32), vmem((NC, 8, RANK), F32),
-            dma((7,)), *gather_sems, dma((4, 8)), dma((2, 9)), dma((2, 2, 9)), dma((4,)),
-            dma((5, NC)), dma((NC,)), dma((2,)),
-        ],
-        compiler_params=pltpu.CompilerParams(collective_id=1, has_side_effects=True, vmem_limit_bytes=60 * 2**20),
-        name="right_factor",
-    )(panel.reshape(ROWS, RANK), thi, tlo)
+    red, lower, own = call(
+        factor_kernel, "sum_and_factor", 2, [(panel, inside), (thi, inside), (tlo, inside)],
+        [gathered, square, chunk],
+        [natural, flat, flat, vmem((2, 8, 2, CA // 2, 128), F32), vmem((2, 8, 2, CA, 128), F32),
+         vmem((2, 9, CA, 128), F32), vmem((2, 2, 9, 2, CB, 128), F32), vmem((4, CB, 128), F32),
+         vmem((RANK, RANK), F32), small, small, small, small, vmem((NC, 4, 8, RANK), F32), vmem((RANK, RANK), F32),
+         dma((7,)), *gather_sems, dma((4, 8)), dma((2, 9)), dma((2, 2, 9)), dma((4,)), dma((5, NC))])
+    half_right = (shape((COLS, RANK), BF16), hbm)
+    thin = (shape((ROWS, RANK), F32), inside)
+    rfh, rfl, basis, update, ownf = call(
+        functools.partial(scale_kernel, n_cols=n_cols, scale=scale), "right_factor", 3,
+        [(panel, inside), (red, inside), (lower, inside), (own, inside)],
+        [half_right, half_right, thin, thin, (shape((CH // 2, RANK), F32), inside)],
+        [vmem((COLS, RANK), BF16), vmem((COLS, RANK), BF16), vmem((8, RANK), F32), vmem((NC, 8, RANK), F32),
+         dma((1,)), dma((NC,)), dma((2,))])
     whole = pl.BlockSpec((ROWS, RANK), lambda b: (0, 0))
-    across = pl.BlockSpec((ROWS, BLK), lambda b: (0, b))
-    down = pl.BlockSpec((BLK, RANK), lambda b: (b, 0))
+    across = pl.BlockSpec((ROWS, HALF), lambda b: (0, b))
+    down = pl.BlockSpec((HALF, RANK), lambda b: (b, 0))
     chunk = pl.BlockSpec((CH // 2, RANK), lambda b: (0, 0))
     return pl.pallas_call(
         output_kernel,
-        grid=(NBLK,),
+        grid=(2,),
         out_shape=(shape((ROWS, COLS), F32), shape((ROWS, COLS), BF16), shape((CH // 2, RANK), F32)),
         in_specs=[across, across, down, down, whole, whole, chunk],
         out_specs=(across, across, chunk),

time: 179 us -> 182 us (1.017)
  Pallas kernels: 178 us -> 181 us
    pallas_call x3 -> x5, Pallas kernels: 178 us -> 181 us  [the longest x4 176 us: call(): pl.pallas_call(body, name=name, out_shape=tuple((o[0] for o in outputs)),...]
where the time goes in v3:
time: 182 us
  Pallas kernels  181 us (99%)
    pallas_call x4, Pallas kernels, call(): pl.pallas_call(body, name=name, out_shape=tuple((o[0] for o in outputs)),...  176 us
    pallas_call x1, Pallas kernels, shards(): pl.pallas_call(output_kernel, grid=(2,), out_shape=(shape((ROWS, COLS), F...  4.63 us

profile of v3, /device:TPU:1, one launch (start us, length us, event | category | flops | bytes accessed | tf_op | source)
XLA Modules:
  0.0 181.8 jit_solution(2191069925571427499)
XLA Ops:
  0.6 46.5 %gather_factor.1 = (f32[6656,128]{1,0:T(8,128)}, bf16[128,3328]{1,0:T(8,128)(2,1)}, bf16[128,3328]{1,0:T(8,128)(2,1)}, bf16[3328,128]{1,0:T(8,128)(2,1)}, bf16[3328,128]{1,0:T(8,128)(2,1)}) custom-call(f32[128,3328]{1,0:T(8,128)} %mom.3, bf16[128,3328]{1,0:T(8,128)(2,1)} %grad.3, f32[52,256]{1,0:T(8,128)} %fac.1), custom_call_target="tpu_custom_call" | custom-call | tf_op jit(solution)/shard_map/gather_factor/pallas_call | solution.py:534
  47.2 22.0 %left_panel.1 = f32[8,16,256]{2,1,0:T(8,128)} custom-call(f32[6656,128]{1,0:T(8,128)} %get-tuple-element.16.gat2, bf16[128,3328]{1,0:T(8,128)(2,1)} %get-tuple-element.17.bhi, bf16[128,3328]{1,0:T(8,128)(2,1)} %get-tuple-element.18.blo), custom_call_target="tpu_custom_call" | custom-call | tf_op jit(solution)/shard_map/left_panel/pallas_call | solution.py:534
  69.1 87.8 %sum_and_factor.1 = (f32[6656,128]{1,0:T(8,128)}, f32[256,256]{1,0:T(8,128)}, f32[104,128]{1,0:T(8,128)}) custom-call(f32[128,256]{1,0:T(8,128)} %bitcast.1, bf16[3328,128]{1,0:T(8,128)(2,1)} %get-tuple-element.19.thi, bf16[3328,128]{1,0:T(8,128)(2,1)} %get-tuple-element.20.tlo), custom_call_target="tpu_custom_call" | custom-call | tf_op jit(solution)/shard_map/sum_and_factor/pallas_call | solution.py:534
  157.0 20.2 %right_factor.1 = (bf16[3328,256]{1,0:T(8,128)(2,1)}, bf16[3328,256]{1,0:T(8,128)(2,1)}, f32[128,256]{1,0:T(8,128)}, f32[128,256]{1,0:T(8,128)}, f32[52,256]{1,0:T(8,128)}) custom-call(f32[128,256]{1,0:T(8,128)} %bitcast.2, f32[6656,128]{1,0:T(8,128)} %get-tuple-element.21.red2, f32[256,256]{1,0:T(8,128)} %get-tuple-element.22.lower, ...), custom_call_target="tpu_custom_call" | custom-call | tf_op jit(solution)/shard_map/right_factor/pallas_call | solution.py:534
  177.2 4.6 %outputs.1 = (f32[128,3328]{1,0:T(8,128)}, bf16[128,3328]{1,0:T(8,128)(2,1)}, f32[52,256]{1,0:T(8,128)}) custom-call(f32[128,3328]{1,0:T(8,128)} %mom.3, bf16[128,3328]{1,0:T(8,128)(2,1)} %grad.3, bf16[3328,256]{1,0:T(8,128)(2,1)} %get-tuple-element.24.rfh, bf16[3328,256]{1,0:T(8,128)(2,1)} %get-tuple-element.25.rfl, f32[128,256]{1,0:T(8,128)} %get-tuple-element.26.basis, ...), custom_call_target="tpu_custom_call" | custom-call | tf_op jit(solution)/shard_map/outputs/pallas_call | solution.py:573

commit v4 on v2

--- a/solution.py
+++ b/solution.py
@@ -23,6 +23,7 @@
 ROWS, COLS, RANK = 128, 3328, 256
 BLK = 256
 NBLK = COLS // BLK
+HALF = COLS // 2
 NB = 32
 
 
@@ -492,9 +493,11 @@
     nt = ((1,), (1,))
     high, low = split(update[...])
     rows = jnp.concatenate([basis[...].astype(BF16), high, low], axis=0)
-    product = dot(rows, rfh[...], nt)
-    momo[...] = mom[...] + grad[...].astype(F32) + product[:ROWS]
-    wupd[...] = (product[ROWS:2 * ROWS] + (product[2 * ROWS:] + dot(high, rfl[...], nt))).astype(BF16)
+    for first in range(0, HALF, BLK):
+        at = slice(first, min(first + BLK, HALF))
+        product = dot(rows, rfh[at, :], nt)
+        momo[:, at] = mom[:, at] + grad[:, at].astype(F32) + product[:ROWS]
+        wupd[:, at] = (product[ROWS:2 * ROWS] + (product[2 * ROWS:] + dot(high, rfl[at, :], nt))).astype(BF16)
 
     @pl.when(pl.program_id(0) == 0)
     def _():
@@ -544,12 +547,12 @@
         name="right_factor",
     )(panel.reshape(ROWS, RANK), thi, tlo)
     whole = pl.BlockSpec((ROWS, RANK), lambda b: (0, 0))
-    across = pl.BlockSpec((ROWS, BLK), lambda b: (0, b))
-    down = pl.BlockSpec((BLK, RANK), lambda b: (b, 0))
+    across = pl.BlockSpec((ROWS, HALF), lambda b: (0, b))
+    down = pl.BlockSpec((HALF, RANK), lambda b: (b, 0))
     chunk = pl.BlockSpec((CH // 2, RANK), lambda b: (0, 0))
     return pl.pallas_call(
         output_kernel,
-        grid=(NBLK,),
+        grid=(2,),
         out_shape=(shape((ROWS, COLS), F32), shape((ROWS, COLS), BF16), shape((CH // 2, RANK), F32)),
         in_specs=[across, across, down, down, whole, whole, chunk],
         out_specs=(across, across, chunk),

time: 179 us -> 173 us (0.966)
  Pallas kernels: 178 us -> 172 us
    pallas_call x1, Pallas kernels: 10.9 us -> 4.63 us  [shards(): pl.pallas_call(output_kernel, grid=(2,), out_shape=(shape((ROWS, COLS), F...]
where the time goes in v4:
time: 173 us
  Pallas kernels  172 us (99%)
    pallas_call x1, Pallas kernels, shards(): pl.pallas_call(functools.partial(factor_kernel, n_cols=n_cols, scale=scal...  104 us
    pallas_call x1, Pallas kernels, shards(): pl.pallas_call(panel_kernel, out_shape=(shape((NC, ROWS // NC, RANK), F32...  63.7 us
    pallas_call x1, Pallas kernels, shards(): pl.pallas_call(output_kernel, grid=(2,), out_shape=(shape((ROWS, COLS), F...  4.63 us

profile of v4, /device:TPU:1, one launch (start us, length us, event | category | flops | bytes accessed | tf_op | source)
XLA Modules:
  0.0 172.6 jit_solution(3011270773909866882)
XLA Ops:
  0.6 63.7 %left_panel.1 = (f32[8,16,256]{2,1,0:T(8,128)}, bf16[3328,128]{1,0:T(8,128)(2,1)}, bf16[3328,128]{1,0:T(8,128)(2,1)}) custom-call(f32[128,3328]{1,0:T(8,128)} %mom.3, bf16[128,3328]{1,0:T(8,128)(2,1)} %grad.3, f32[52,256]{1,0:T(8,128)} %fac.1), custom_call_target="tpu_custom_call" | custom-call | tf_op jit(solution)/shard_map/left_panel/pallas_call | solution.py:517
  64.3 103.6 %right_factor.1 = (bf16[3328,256]{1,0:T(8,128)(2,1)}, bf16[3328,256]{1,0:T(8,128)(2,1)}, f32[128,256]{1,0:T(8,128)}, f32[128,256]{1,0:T(8,128)}, f32[52,256]{1,0:T(8,128)}) custom-call(f32[128,256]{1,0:T(8,128)} %bitcast.1, bf16[3328,128]{1,0:T(8,128)(2,1)} %get-tuple-element.12.thi, bf16[3328,128]{1,0:T(8,128)(2,1)} %get-tuple-element.13.tlo), custom_call_target="tpu_custom_call" | custom-call | tf_op jit(solution)/shard_map/right_factor/pallas_call | solution.py:530
  167.9 4.6 %outputs.1 = (f32[128,3328]{1,0:T(8,128)}, bf16[128,3328]{1,0:T(8,128)(2,1)}, f32[52,256]{1,0:T(8,128)}) custom-call(f32[128,3328]{1,0:T(8,128)} %mom.3, bf16[128,3328]{1,0:T(8,128)(2,1)} %grad.3, bf16[3328,256]{1,0:T(8,128)(2,1)} %get-tuple-element.14.rfh, bf16[3328,256]{1,0:T(8,128)(2,1)} %get-tuple-element.15.rfl, f32[128,256]{1,0:T(8,128)} %get-tuple-element.16.basis, ...), custom_call_target="tpu_custom_call" | custom-call | tf_op jit(solution)/shard_map/outputs/pallas_call | solution.py:553

commit v5 on v4

--- a/solution.py
+++ b/solution.py
@@ -51,10 +51,17 @@
         self.x, self.z = self.r // NZ, self.r % NZ
 
         x, z, c = self.x, self.z, self.c
-        self.xs = {d: {"row": lax.rem(x + d, NX) * NZ + z, "col": c} for d in (1, 2, 3)}
-        self.zs = {d: {"row": x * NZ + lax.rem(z + d, NZ), "col": c} for d in (1, 4, 8, 12, 15)}
+        self.sign = 1 - 2 * lax.rem(c, 2)
+        self.xs = {d: {"row": self.to_x(d) * NZ + z, "col": c} for d in (1, 2, 3)}
+        self.zs = {d: {"row": x * NZ + self.to_z(d), "col": c} for d in (1, 4, 8, 12, 15)}
         self.qs = {d: {"row": x * NZ + (z // 4) * 4 + lax.rem(z + d, 4), "col": c} for d in (1, 2, 3)}
         self.cs = {d: {"row": self.r, "col": lax.rem(c + d, NC)} for d in range(1, NC)}
+
+    def to_x(self, d):
+        return lax.rem(self.x + self.sign * d + NX, NX)
+
+    def to_z(self, d):
+        return lax.rem(self.z + self.sign * d + NZ, NZ)
 
     def copy(self, src, dst, recv, device, slot=0):
         return pltpu.make_async_remote_copy(
@@ -86,7 +93,7 @@
     return tuple(jnp.concatenate(p, axis=1) for p in zip(*parts))
 
 
-def gather(t, buf, natural, sems, work):
+def gather(t, buf, natural, sems, work, before_b=lambda: None):
     agaz, agax, agbx, agbz = sems
     xs, send, recv = t.xs, t.send, t.recv
     right, left = t.zs[1], t.zs[15]
@@ -115,10 +122,11 @@
         recv(two(2, k, n, 0, half), agax.at[2, s])
         recv(two(2, k, n, half, half), agax.at[3, s])
 
+    send(one(0), one(1), agaz.at[0, 1], right, 0)
+    send(one(0), one(2), agaz.at[1, 1], left, 0)
+    before_b()
     for d in (1, 2, 3):
         send(buf.at[0, 0, pl.ds(CA, CB)], buf.at[d, 0, pl.ds(CA, CB)], agbx.at[d], xs[d], 0)
-    send(one(0), one(1), agaz.at[0, 1], right, 0)
-    send(one(0), one(2), agaz.at[1, 1], left, 0)
     side(0, 1, 0)
     for d in (1, 2, 3):
         recv(buf.at[d, 0, pl.ds(CA, CB)], agbx.at[d])
@@ -171,25 +179,30 @@
     finish(15, 1, 8)
     t.sent(buf.reshape(NX * NZ * CH, 128).at[pl.ds(0, 6552)], 0)
 
-    def place(n, carry):
-        s = lax.rem(t.z - n + 2 * NZ, NZ)
+    def place(s, carry):
         k = jnp.where(s == 0, 0, jnp.where(s > 8, 2 * (NZ - s), 2 * s - 1))
+        n = t.to_z(-s)
         for i in range(NX):
-            row = lax.rem(t.x - i + NX, NX) * NZ + n
+            row = t.to_x(-i) * NZ + n
             natural[pl.ds(pl.multiple_of(CH * row, 8), CH), :] = buf[i, k]
         return carry
 
     lax.fori_loop(0, NZ, place, 0)
 
 
-def panel_kernel(mom, grad, fac, panel, thi, tlo, momv, gradv, bhi, blo, gat, gat2, ppart, precv,
-                 lsem, ssem, agaz, agax, agbx, agbz, psem):
+def factor_kernel(mom, grad, fac, rfh, rfl, basis, update, ownf,
+                  momv, gradv, bhi, blo, thi, tlo, gat, gat2, ppart, precv, panel,
+                  term, part, red, red2, xh, xf, za, zb, xb, gram, g0, g1, g2, g3, g4, aw, rfhv, rflv, sq, sqr,
+                  lsem, ssem, tsem, agaz, agax, agbx, agbz, bgaz, bgax, bgbx, bgbz, psem,
+                  rsx, rsza, rszb, rsxb, gsem, qsem, osem, *, n_cols, scale):
     t = Links(ssem, agbx.at[0])
-    c, cs, send, recv, sent = t.c, t.cs, t.send, t.recv, t.sent
+    t2 = Links(tsem, agbx.at[0])
+    r, c, x, z = t.r, t.c, t.x, t.z
+    xs, zs, qs, cs, send, recv, sent = t.xs, t.zs, t.qs, t.cs, t.send, t.recv, t.sent
     loads = (pltpu.make_async_copy(mom, momv, lsem.at[0]), pltpu.make_async_copy(grad, gradv, lsem.at[1]))
     for load in loads:
         load.start()
-    greeted = t.greet([*t.xs.values(), *cs.values(), t.zs[1], t.zs[15]])
+    greeted = t.greet([*xs.values(), *zs.values(), *qs.values(), *cs.values()])
 
     gat.at[0, 0][pl.ds(0, CH // 2, stride=2), :] = fac[:, :128]
     gat.at[0, 0][pl.ds(1, CH // 2, stride=2), :] = fac[:, 128:]
@@ -236,24 +249,14 @@
         recv(panel.at[lax.rem(c - d + NC, NC)], psem.at[1, d])
     sent(gat2.at[pl.ds(0, 14 * 32)], 1)
 
-
-def factor_kernel(panel, thi, tlo, rfh, rfl, basis, update, ownf,
-                  term, part, red, red2, xh, xf, za, zb, xb, gram, g0, g1, g2, g3, g4, aw, rfhv, rflv, sq, sqr,
-                  ssem, agaz, agax, agbx, agbz, rsx, rsza, rszb, rsxb, gsem, qsem, osem, *, n_cols, scale):
-    t = Links(ssem, agbx.at[0])
-    r, c, x, z = t.r, t.c, t.x, t.z
-    xs, zs, qs, cs, send, recv, sent = t.xs, t.zs, t.qs, t.cs, t.send, t.recv, t.sent
-    greeted = t.greet([*xs.values(), *zs.values(), *qs.values(), *cs.values()])
-
-    left = panel[...]
+    left = panel[...].reshape(ROWS, RANK)
     gram[...] = dot6(left.T, left)
-    greeted()
 
     def gram_rows(xi):
         return pl.ds(pl.multiple_of(32 * c + 8 * xi, 8), 8)
 
     for d in (1, 2, 3):
-        send(gram.at[gram_rows(lax.rem(x + d, NX))], g0.at[d], gsem.at[0, d], xs[d], 2)
+        send(gram.at[gram_rows(t.to_x(d))], g0.at[d], gsem.at[0, d], xs[d], 2)
 
     def gram_0():
         total = gram[gram_rows(x), :]
@@ -284,7 +287,7 @@
 
     def gram_3():
         for d in (1, 2, 3):
-            recv(g3.at[lax.rem(x - d + NX, NX)], gsem.at[3, d])
+            recv(g3.at[t.to_x(-d)], gsem.at[3, d])
         g4[c] = g3[...]
         for d in range(1, NC):
             send(g4.at[c], g4.at[c], gsem.at[4, d], cs[d], 3)
@@ -342,9 +345,9 @@
     gram_1()
 
     def place(k, carry):
-        n = lax.rem(jnp.where(lax.rem(k, 2) == 0, z + 8 - k // 2, jnp.where(k == 15, z, z + 9 + k // 2)), NZ)
+        n = t.to_z(jnp.where(k == 15, 0, jnp.where(lax.rem(k, 2) == 0, 8 - k // 2, k // 2 - 7)))
         for i in range(NX):
-            row = lax.rem(x + i, NX) * NZ + n
+            row = t.to_x(i) * NZ + n
             part[i, k] = term[pl.ds(pl.multiple_of(CH * row, 8), CH), :]
         return carry
 
@@ -444,19 +447,21 @@
     recv(za.at[0, 8], rsza.at[0, 8])
     recv(za.at[1, 7], rsza.at[1, 7])
     red[0, 0, :CA, :] = part[0, 15, :CA, :] + (za[0, 8] + za[1, 7])
-    total = part[0, 15, CA:, :]
-    for d in (1, 2, 3):
-        recv(xb.at[d], rsxb.at[d])
-        total = total + xb[d]
-    red[0, 0, CA:, :] = total
-    sent(term.at[pl.ds(0, 6552)], 4)
+
+    def finish_b():
+        total = part[0, 15, CA:, :]
+        for d in (1, 2, 3):
+            recv(xb.at[d], rsxb.at[d])
+            total = total + xb[d]
+        red[0, 0, CA:, :] = total
 
     def factor_rest(s):
         @pl.when(s < 4)
         def _():
             factor_block(s + 4)
 
-    gather(t, red, red2, (agaz, agax, agbx, agbz), factor_rest)
+    gather(t2, red, red2, (bgaz, bgax, bgbx, bgbz), factor_rest, finish_b)
+    sent(term.at[pl.ds(0, 6552)], 4)
 
     inverse = jnp.where(i_all >= j_all, aw[...], 0.0)
     nt = ((1,), (1,))
@@ -514,38 +519,27 @@
     flat, natural = vmem((NX, NZ, CH, 128), F32), vmem((NX * NZ * CH, 128), F32)
     gather_sems = [dma((2, 9)), dma((4, 9)), dma((4,)), dma((2, 2, 9))]
     rows16 = vmem((NC, ROWS // NC, RANK), F32)
-    panel, thi, tlo = pl.pallas_call(
-        panel_kernel,
-        out_shape=(shape((NC, ROWS // NC, RANK), F32), shape((COLS, ROWS), BF16), shape((COLS, ROWS), BF16)),
-        in_specs=[hbm, hbm, inside],
-        out_specs=(inside, inside, inside),
-        scratch_shapes=[
-            vmem((ROWS, COLS), F32), vmem((ROWS, COLS), BF16), vmem((ROWS, COLS), BF16), vmem((ROWS, COLS), BF16),
-            flat, natural, rows16, rows16, dma((2,)), dma((2,)), *gather_sems, dma((2, NC)),
-        ],
-        compiler_params=pltpu.CompilerParams(collective_id=0, has_side_effects=True, vmem_limit_bytes=60 * 2**20),
-        name="left_panel",
-    )(momentum, gradient, factor)
     small = vmem((4, 8, RANK), F32)
+    wide, tall, full = vmem((ROWS, COLS), BF16), vmem((COLS, ROWS), BF16), vmem((COLS, RANK), BF16)
     rfh, rfl, basis, update, ownf = pl.pallas_call(
         functools.partial(factor_kernel, n_cols=n_cols, scale=scale),
         out_shape=(
             shape((COLS, RANK), BF16), shape((COLS, RANK), BF16),
             shape((ROWS, RANK), F32), shape((ROWS, RANK), F32), shape((CH // 2, RANK), F32)),
-        in_specs=[inside, inside, inside],
+        in_specs=[hbm, hbm, inside],
         out_specs=(hbm, hbm, inside, inside, inside),
         scratch_shapes=[
+            vmem((ROWS, COLS), F32), wide, wide, wide, tall, tall, flat, natural, rows16, rows16, rows16,
             natural, flat, flat, natural, vmem((2, 8, 2, CA // 2, 128), F32), vmem((2, 8, 2, CA, 128), F32),
             vmem((2, 9, CA, 128), F32), vmem((2, 2, 9, 2, CB, 128), F32), vmem((4, CB, 128), F32),
             vmem((RANK, RANK), F32), small, small, small, small, vmem((NC, 4, 8, RANK), F32),
-            vmem((RANK, RANK), F32), vmem((COLS, RANK), BF16), vmem((COLS, RANK), BF16),
-            vmem((8, RANK), F32), vmem((NC, 8, RANK), F32),
-            dma((7,)), *gather_sems, dma((4, 8)), dma((2, 9)), dma((2, 2, 9)), dma((4,)),
-            dma((5, NC)), dma((NC,)), dma((2,)),
+            vmem((RANK, RANK), F32), full, full, vmem((8, RANK), F32), vmem((NC, 8, RANK), F32),
+            dma((2,)), dma((7,)), dma((1,)), *gather_sems, *gather_sems, dma((2, NC)),
+            dma((4, 8)), dma((2, 9)), dma((2, 2, 9)), dma((4,)), dma((5, NC)), dma((NC,)), dma((2,)),
         ],
-        compiler_params=pltpu.CompilerParams(collective_id=1, has_side_effects=True, vmem_limit_bytes=60 * 2**20),
+        compiler_params=pltpu.CompilerParams(collective_id=0, has_side_effects=True, vmem_limit_bytes=60 * 2**20),
         name="right_factor",
-    )(panel.reshape(ROWS, RANK), thi, tlo)
+    )(momentum, gradient, factor)
     whole = pl.BlockSpec((ROWS, RANK), lambda b: (0, 0))
     across = pl.BlockSpec((ROWS, HALF), lambda b: (0, b))
     down = pl.BlockSpec((HALF, RANK), lambda b: (b, 0))

time: 173 us -> 167 us (0.965)
  Pallas kernels: 172 us -> 166 us
    pallas_call x1 -> x0, Pallas kernels: 63.7 us -> none  [shards(): pl.pallas_call(panel_kernel, out_shape=(shape((NC, ROWS // NC, RANK), F32...]
    pallas_call x1, Pallas kernels: 104 us -> 161 us  [shards(): pl.pallas_call(functools.partial(factor_kernel, n_cols=n_cols, scale=scal...]
where the time goes in v5:
time: 167 us
  Pallas kernels  166 us (99%)
    pallas_call x1, Pallas kernels, shards(): pl.pallas_call(functools.partial(factor_kernel, n_cols=n_cols, scale=scal...  161 us
    pallas_call x1, Pallas kernels, shards(): pl.pallas_call(output_kernel, grid=(2,), out_shape=(shape((ROWS, COLS), F...  4.63 us

profile of v5, /device:TPU:1, one launch (start us, length us, event | category | flops | bytes accessed | tf_op | source)
XLA Modules:
  0.0 166.6 jit_solution(12698766830361782468)
XLA Ops:
  0.6 161.3 %right_factor.1 = (bf16[3328,256]{1,0:T(8,128)(2,1)}, bf16[3328,256]{1,0:T(8,128)(2,1)}, f32[128,256]{1,0:T(8,128)}, f32[128,256]{1,0:T(8,128)}, f32[52,256]{1,0:T(8,128)}) custom-call(f32[128,3328]{1,0:T(8,128)} %mom.3, bf16[128,3328]{1,0:T(8,128)(2,1)} %grad.3, f32[52,256]{1,0:T(8,128)} %fac.1), custom_call_target="tpu_custom_call" | custom-call | tf_op jit(solution)/shard_map/right_factor/pallas_call | solution.py:524
  162.0 4.6 %outputs.1 = (f32[128,3328]{1,0:T(8,128)}, bf16[128,3328]{1,0:T(8,128)(2,1)}, f32[52,256]{1,0:T(8,128)}) custom-call(f32[128,3328]{1,0:T(8,128)} %mom.3, bf16[128,3328]{1,0:T(8,128)(2,1)} %grad.3, bf16[3328,256]{1,0:T(8,128)(2,1)} %get-tuple-element.8.rfh, bf16[3328,256]{1,0:T(8,128)(2,1)} %get-tuple-element.9.rfl, f32[128,256]{1,0:T(8,128)} %get-tuple-element.10.basis, ...), custom_call_target="tpu_custom_call" | custom-call | tf_op jit(solution)/shard_map/outputs/pallas_call | solution.py:547

commit v6 on v5

--- a/solution.py
+++ b/solution.py
@@ -18,7 +18,7 @@
 NX, NZ = 4, 16
 NC = 8
 CH = 104
-CA = 64
+CA = 80
 CB = CH - CA
 ROWS, COLS, RANK = 128, 3328, 256
 BLK = 256
@@ -53,7 +53,7 @@
         x, z, c = self.x, self.z, self.c
         self.sign = 1 - 2 * lax.rem(c, 2)
         self.xs = {d: {"row": self.to_x(d) * NZ + z, "col": c} for d in (1, 2, 3)}
-        self.zs = {d: {"row": x * NZ + self.to_z(d), "col": c} for d in (1, 4, 8, 12, 15)}
+        self.zs = {d: {"row": x * NZ + self.to_z(d), "col": c} for d in (1, 4, 5, 8, 11, 12, 15)}
         self.qs = {d: {"row": x * NZ + (z // 4) * 4 + lax.rem(z + d, 4), "col": c} for d in (1, 2, 3)}
         self.cs = {d: {"row": self.r, "col": lax.rem(c + d, NC)} for d in range(1, NC)}
 
@@ -93,110 +93,124 @@
     return tuple(jnp.concatenate(p, axis=1) for p in zip(*parts))
 
 
+SLOT = {0: 0, 1: 1, 15: 2, 5: 3, 11: 4, 2: 5, 14: 6, 6: 7, 10: 8, 4: 9, 12: 10, 7: 11, 9: 12, 3: 13, 13: 14, 8: 15}
+GROUPS = ((0, 1), (1, 2), (3, 2), (5, 2), (7, 4), (11, 4), (15, 1))
+
+
 def gather(t, buf, natural, sems, work, before_b=lambda: None):
-    agaz, agax, agbx, agbz = sems
+    zsem, xsem, bsem, bxsem = sems
     xs, send, recv = t.xs, t.send, t.recv
-    right, left = t.zs[1], t.zs[15]
+    right, left, far_right, far_left = t.zs[1], t.zs[15], t.zs[5], t.zs[11]
     half = CA // 2
 
-    def one(k):
-        return buf.at[0, k, pl.ds(0, CA)]
-
-    def two(i, k, n, lo=0, size=CA):
-        return buf.at[i, pl.ds(k, n), pl.ds(lo, size)]
-
-    def group(g, k):
-        return buf.at[pl.ds(2 * g, 2), k, pl.ds(CA, CB)]
-
-    def side(k, n, s):
-        send(two(0, k, n), two(1, k, n), agax.at[0, s], xs[1], 0)
-        send(two(0, k, n), two(3, k, n), agax.at[1, s], xs[3], 0)
-
-    def forward(k, n, s):
-        recv(two(1, k, n), agax.at[0, s])
-        send(two(1, k, n, 0, half), two(2, k, n, 0, half), agax.at[2, s], xs[1], 0)
-        recv(two(3, k, n), agax.at[1, s])
-        send(two(3, k, n, half, half), two(2, k, n, half, half), agax.at[3, s], xs[3], 0)
-
-    def finish(k, n, s):
-        recv(two(2, k, n, 0, half), agax.at[2, s])
-        recv(two(2, k, n, half, half), agax.at[3, s])
-
-    send(one(0), one(1), agaz.at[0, 1], right, 0)
-    send(one(0), one(2), agaz.at[1, 1], left, 0)
+    def one(k, lo=0, size=CA):
+        return buf.at[0, k, pl.ds(lo, size)]
+
+    def four(k):
+        return buf.at[pl.ds(0, NX), k, pl.ds(CA, CB)]
+
+    def many(i, g, lo=0, size=CA):
+        return buf.at[i, pl.ds(GROUPS[g][0], GROUPS[g][1]), pl.ds(lo, size)]
+
+    def pass_a(k, *ways):
+        if k:
+            recv(one(k), zsem.at[k])
+        for to, device in ways:
+            send(one(k), one(to), zsem.at[to], device, 0)
+
+    def pass_b(k, *ways):
+        if k:
+            recv(four(k), bsem.at[k])
+        for to, device in ways:
+            send(four(k), four(to), bsem.at[to], device, 0)
+
+    def side(g):
+        send(many(0, g), many(1, g), xsem.at[0, g], xs[1], 0)
+        send(many(0, g), many(3, g), xsem.at[1, g], xs[3], 0)
+
+    def forward(g):
+        recv(many(1, g), xsem.at[0, g])
+        send(many(1, g, 0, half), many(2, g, 0, half), xsem.at[2, g], xs[1], 0)
+        recv(many(3, g), xsem.at[1, g])
+        send(many(3, g, half, half), many(2, g, half, half), xsem.at[3, g], xs[3], 0)
+
+    pass_a(0, (3, far_right), (4, far_left), (1, right), (2, left))
     before_b()
     for d in (1, 2, 3):
-        send(buf.at[0, 0, pl.ds(CA, CB)], buf.at[d, 0, pl.ds(CA, CB)], agbx.at[d], xs[d], 0)
-    side(0, 1, 0)
+        send(buf.at[0, 0, pl.ds(CA, CB)], buf.at[d, 0, pl.ds(CA, CB)], bxsem.at[d], xs[d], 0)
+    side(0)
     for d in (1, 2, 3):
-        recv(buf.at[d, 0, pl.ds(CA, CB)], agbx.at[d])
-    for g in (0, 1):
-        send(group(g, 0), group(g, 1), agbz.at[0, g, 1], right, 0)
-        send(group(g, 0), group(g, 2), agbz.at[1, g, 1], left, 0)
-    forward(0, 1, 0)
-
-    def step(s, carry):
-        kr, kl = 2 * s - 1, 2 * s
-        recv(one(kr), agaz.at[0, s])
-        send(one(kr), one(kr + 2), agaz.at[0, s + 1], right, 0)
-        recv(one(kl), agaz.at[1, s])
-
-        @pl.when(s < 7)
-        def _():
-            send(one(kl), one(kl + 2), agaz.at[1, s + 1], left, 0)
-
-        side(kr, 2, s)
-        for g in (0, 1):
-            recv(group(g, kl), agbz.at[1, g, s])
-            send(group(g, kl), group(g, jnp.minimum(kl + 2, 15)), agbz.at[1, g, s + 1], left, 0)
-            recv(group(g, kr), agbz.at[0, g, s])
-
-            @pl.when(s < 7)
-            def _():
-                send(group(g, kr), group(g, kr + 2), agbz.at[0, g, s + 1], right, 0)
-
-        @pl.when(s > 1)
-        def _():
-            forward(kr - 2, 2, s - 1)
-
-        work(s)
-        return carry
-
-    lax.fori_loop(1, 8, step, 0)
-    recv(one(15), agaz.at[0, 8])
-    side(15, 1, 8)
-    forward(13, 2, 7)
-    for g in (0, 1):
-        recv(group(g, 15), agbz.at[1, g, 8])
-    forward(15, 1, 8)
-    finish(0, 1, 0)
-
-    def last(s, carry):
-        finish(2 * s - 1, 2, s)
-        return carry
-
-    lax.fori_loop(1, 8, last, 0)
-    finish(15, 1, 8)
-    t.sent(buf.reshape(NX * NZ * CH, 128).at[pl.ds(0, 6552)], 0)
-
-    def place(s, carry):
-        k = jnp.where(s == 0, 0, jnp.where(s > 8, 2 * (NZ - s), 2 * s - 1))
-        n = t.to_z(-s)
+        recv(buf.at[d, 0, pl.ds(CA, CB)], bxsem.at[d])
+    pass_b(0, (3, far_right), (4, far_left), (1, right), (2, left))
+    work(0)
+    pass_a(1, (5, right))
+    pass_a(2, (6, left))
+    side(1)
+    forward(0)
+    pass_a(3, (7, right), (9, left))
+    pass_a(4, (8, left), (10, right))
+    side(2)
+    pass_b(1, (5, right))
+    pass_b(2, (6, left))
+    work(1)
+    pass_b(3, (7, right), (9, left))
+    pass_b(4, (8, left), (10, right))
+    forward(1)
+    pass_a(5)
+    pass_a(6)
+    side(3)
+    pass_a(7, (11, right))
+    pass_a(8, (12, left))
+    pass_a(9, (13, left))
+    pass_a(10, (14, right))
+    side(4)
+    forward(2)
+    pass_b(5)
+    pass_b(6)
+    pass_b(7, (11, right))
+    pass_b(8, (12, left))
+    pass_b(9, (13, left))
+    pass_b(10, (14, right))
+    work(2)
+    forward(3)
+    pass_a(11)
+    pass_a(12)
+    send(one(11, 0, half), one(15, 0, half), zsem.at[15], right, 0)
+    send(one(12, half, half), one(15, half, half), zsem.at[16], left, 0)
+    pass_a(13)
+    pass_a(14)
+    side(5)
+    pass_b(11)
+    pass_b(12, (15, left))
+    forward(4)
+    recv(one(15, 0, half), zsem.at[15])
+    recv(one(15, half, half), zsem.at[16])
+    side(6)
+    pass_b(13)
+    pass_b(14)
+    work(3)
+    forward(5)
+    forward(6)
+    pass_b(15)
+    for g in range(len(GROUPS)):
+        recv(many(2, g, 0, half), xsem.at[2, g])
+        recv(many(2, g, half, half), xsem.at[3, g])
+    t.sent(natural.at[pl.ds(0, 6552)], 0)
+
+    for d, k in SLOT.items():
+        n = t.to_z(-d)
         for i in range(NX):
             row = t.to_x(-i) * NZ + n
             natural[pl.ds(pl.multiple_of(CH * row, 8), CH), :] = buf[i, k]
-        return carry
-
-    lax.fori_loop(0, NZ, place, 0)
 
 
 def factor_kernel(mom, grad, fac, rfh, rfl, basis, update, ownf,
                   momv, gradv, bhi, blo, thi, tlo, gat, gat2, ppart, precv, panel,
                   term, part, red, red2, xh, xf, za, zb, xb, gram, g0, g1, g2, g3, g4, aw, rfhv, rflv, sq, sqr,
-                  lsem, ssem, tsem, agaz, agax, agbx, agbz, bgaz, bgax, bgbx, bgbz, psem,
+                  lsem, ssem, tsem, agaz, agax, agbz, agbx, bgaz, bgax, bgbz, bgbx, psem,
                   rsx, rsza, rszb, rsxb, gsem, qsem, osem, *, n_cols, scale):
-    t = Links(ssem, agbx.at[0])
-    t2 = Links(tsem, agbx.at[0])
+    t = Links(ssem, psem.at[0, 0])
+    t2 = Links(tsem, psem.at[0, 0])
     r, c, x, z = t.r, t.c, t.x, t.z
     xs, zs, qs, cs, send, recv, sent = t.xs, t.zs, t.qs, t.cs, t.send, t.recv, t.sent
     loads = (pltpu.make_async_copy(mom, momv, lsem.at[0]), pltpu.make_async_copy(grad, gradv, lsem.at[1]))
@@ -216,19 +230,18 @@
         high, low = split(value.T)
         thi[at, :], tlo[at, :] = high, low
 
-    def prepare_step(s):
-        @pl.when(s == 1)
-        def _():
+    def prepare_some(i):
+        if i == 0:
             for load in loads:
                 load.wait()
 
-        prepare(2 * s - 2)
-
-        @pl.when(s < 7)
-        def _():
-            prepare(2 * s - 1)
-
-    gather(t, gat, gat2, (agaz, agax, agbx, agbz), prepare_step)
+        def step(b, carry):
+            prepare(b)
+            return carry
+
+        lax.fori_loop(*((0, 3), (3, 6), (6, 10), (10, NBLK))[i], step, 0)
+
+    gather(t, gat, gat2, (agaz, agax, agbz, agbx), prepare_some)
 
     def panel_step(b, total):
         at = block(b)
@@ -455,12 +468,11 @@
             total = total + xb[d]
         red[0, 0, CA:, :] = total
 
-    def factor_rest(s):
-        @pl.when(s < 4)
-        def _():
-            factor_block(s + 4)
-
-    gather(t2, red, red2, (bgaz, bgax, bgbx, bgbz), factor_rest, finish_b)
+    def factor_rest(i):
+        if i:
+            factor_block(jnp.int32(i + 4))
+
+    gather(t2, red, red2, (bgaz, bgax, bgbz, bgbx), factor_rest, finish_b)
     sent(term.at[pl.ds(0, 6552)], 4)
 
     inverse = jnp.where(i_all >= j_all, aw[...], 0.0)
@@ -517,7 +529,7 @@
     inside = pl.BlockSpec(memory_space=pltpu.VMEM)
     shape = jax.ShapeDtypeStruct
     flat, natural = vmem((NX, NZ, CH, 128), F32), vmem((NX * NZ * CH, 128), F32)
-    gather_sems = [dma((2, 9)), dma((4, 9)), dma((4,)), dma((2, 2, 9))]
+    gather_sems = [dma((17,)), dma((4, 7)), dma((16,)), dma((4,))]
     rows16 = vmem((NC, ROWS // NC, RANK), F32)
     small = vmem((4, 8, RANK), F32)
     wide, tall, full = vmem((ROWS, COLS), BF16), vmem((COLS, ROWS), BF16), vmem((COLS, RANK), BF16)

time: 167 us -> 159 us (0.952)
  Pallas kernels: 166 us -> 158 us
    pallas_call x1, Pallas kernels: 161 us -> 154 us  [shards(): pl.pallas_call(functools.partial(factor_kernel, n_cols=n_cols, scale=scal...]
where the time goes in v6:
time: 159 us
  Pallas kernels  158 us (99%)
    pallas_call x1, Pallas kernels, shards(): pl.pallas_call(functools.partial(factor_kernel, n_cols=n_cols, scale=scal...  154 us
    pallas_call x1, Pallas kernels, shards(): pl.pallas_call(output_kernel, grid=(2,), out_shape=(shape((ROWS, COLS), F...  4.63 us

profile of v6, /device:TPU:1, one launch (start us, length us, event | category | flops | bytes accessed | tf_op | source)
XLA Modules:
  0.0 158.9 jit_solution(15097828797336688060)
XLA Ops:
  0.6 153.7 %right_factor.1 = (bf16[3328,256]{1,0:T(8,128)(2,1)}, bf16[3328,256]{1,0:T(8,128)(2,1)}, f32[128,256]{1,0:T(8,128)}, f32[128,256]{1,0:T(8,128)}, f32[52,256]{1,0:T(8,128)}) custom-call(f32[128,3328]{1,0:T(8,128)} %mom.3, bf16[128,3328]{1,0:T(8,128)(2,1)} %grad.3, f32[52,256]{1,0:T(8,128)} %fac.1), custom_call_target="tpu_custom_call" | custom-call | tf_op jit(solution)/shard_map/right_factor/pallas_call | solution.py:536
  154.3 4.6 %outputs.1 = (f32[128,3328]{1,0:T(8,128)}, bf16[128,3328]{1,0:T(8,128)(2,1)}, f32[52,256]{1,0:T(8,128)}) custom-call(f32[128,3328]{1,0:T(8,128)} %mom.3, bf16[128,3328]{1,0:T(8,128)(2,1)} %grad.3, bf16[3328,256]{1,0:T(8,128)(2,1)} %get-tuple-element.8.rfh, bf16[3328,256]{1,0:T(8,128)(2,1)} %get-tuple-element.9.rfl, f32[128,256]{1,0:T(8,128)} %get-tuple-element.10.basis, ...), custom_call_target="tpu_custom_call" | custom-call | tf_op jit(solution)/shard_map/outputs/pallas_call | solution.py:559

commit v7 on v6

--- a/solution.py
+++ b/solution.py
@@ -94,7 +94,7 @@
 
 
 SLOT = {0: 0, 1: 1, 15: 2, 5: 3, 11: 4, 2: 5, 14: 6, 6: 7, 10: 8, 4: 9, 12: 10, 7: 11, 9: 12, 3: 13, 13: 14, 8: 15}
-GROUPS = ((0, 1), (1, 2), (3, 2), (5, 2), (7, 4), (11, 4), (15, 1))
+GROUPS = ((0, 1), (1, 2), (3, 2), (5, 2), (7, 2), (9, 2), (11, 2), (13, 2), (15, 1))
 
 
 def gather(t, buf, natural, sems, work, before_b=lambda: None):
@@ -161,9 +161,10 @@
     side(3)
     pass_a(7, (11, right))
     pass_a(8, (12, left))
+    side(4)
     pass_a(9, (13, left))
     pass_a(10, (14, right))
-    side(4)
+    side(5)
     forward(2)
     pass_b(5)
     pass_b(6)
@@ -173,26 +174,31 @@
     pass_b(10, (14, right))
     work(2)
     forward(3)
+    forward(4)
     pass_a(11)
     pass_a(12)
     send(one(11, 0, half), one(15, 0, half), zsem.at[15], right, 0)
     send(one(12, half, half), one(15, half, half), zsem.at[16], left, 0)
+    side(6)
     pass_a(13)
     pass_a(14)
-    side(5)
+    side(7)
     pass_b(11)
     pass_b(12, (15, left))
-    forward(4)
+    forward(5)
     recv(one(15, 0, half), zsem.at[15])
     recv(one(15, half, half), zsem.at[16])
-    side(6)
+    side(8)
+    send(many(0, 8), many(2, 8), xsem.at[2, 8], xs[2], 0)
     pass_b(13)
     pass_b(14)
     work(3)
-    forward(5)
     forward(6)
+    forward(7)
     pass_b(15)
-    for g in range(len(GROUPS)):
+    for i, way in ((1, 0), (3, 1), (2, 2)):
+        recv(many(i, 8), xsem.at[way, 8])
+    for g in range(len(GROUPS) - 1):
         recv(many(2, g, 0, half), xsem.at[2, g])
         recv(many(2, g, half, half), xsem.at[3, g])
     t.sent(natural.at[pl.ds(0, 6552)], 0)
@@ -205,7 +211,7 @@
 
 
 def factor_kernel(mom, grad, fac, rfh, rfl, basis, update, ownf,
-                  momv, gradv, bhi, blo, thi, tlo, gat, gat2, ppart, precv, panel,
+                  momv, gradv, bhi, blo, th, gat, gat2, ppart, precv, panel,
                   term, part, red, red2, xh, xf, za, zb, xb, gram, g0, g1, g2, g3, g4, aw, rfhv, rflv, sq, sqr,
                   lsem, ssem, tsem, agaz, agax, agbz, agbx, bgaz, bgax, bgbz, bgbx, psem,
                   rsx, rsza, rszb, rsxb, gsem, qsem, osem, *, n_cols, scale):
@@ -227,8 +233,7 @@
         value = momv[:, at] + gradv[:, at].astype(F32)
         high, low = split(value)
         bhi[:, at], blo[:, at] = high, low
-        high, low = split(value.T)
-        thi[at, :], tlo[at, :] = high, low
+        th[at, :ROWS], th[at, ROWS:] = split(value.T)
 
     def prepare_some(i):
         if i == 0:
@@ -345,10 +350,11 @@
         aw[...] = jnp.where(done, 0.0, aw[...]) - dot6(below.T, rows)
         aw[pl.ds(first, NB), :] = rows
 
-    lp = split(left)
+    lp_high, lp_low = split(left)
+    lp_twice = jnp.concatenate([lp_high, lp_high], axis=0)
 
     def term_step(b, carry):
-        h = dot3((thi[block(b), :], tlo[block(b), :]), lp)
+        h = dot(th[block(b), :], lp_twice) + dot(th[block(b), :ROWS], lp_low)
         term[pl.ds(2 * BLK * b, BLK, stride=2), :] = h[:, :128]
         term[pl.ds(2 * BLK * b + 1, BLK, stride=2), :] = h[:, 128:]
         pl.when(b == 6)(gram_0)
@@ -529,10 +535,10 @@
     inside = pl.BlockSpec(memory_space=pltpu.VMEM)
     shape = jax.ShapeDtypeStruct
     flat, natural = vmem((NX, NZ, CH, 128), F32), vmem((NX * NZ * CH, 128), F32)
-    gather_sems = [dma((17,)), dma((4, 7)), dma((16,)), dma((4,))]
+    gather_sems = [dma((17,)), dma((4, 9)), dma((16,)), dma((4,))]
     rows16 = vmem((NC, ROWS // NC, RANK), F32)
     small = vmem((4, 8, RANK), F32)
-    wide, tall, full = vmem((ROWS, COLS), BF16), vmem((COLS, ROWS), BF16), vmem((COLS, RANK), BF16)
+    wide, tall, full = vmem((ROWS, COLS), BF16), vmem((COLS, 2 * ROWS), BF16), vmem((COLS, RANK), BF16)
     rfh, rfl, basis, update, ownf = pl.pallas_call(
         functools.partial(factor_kernel, n_cols=n_cols, scale=scale),
         out_shape=(
@@ -541,7 +547,7 @@
         in_specs=[hbm, hbm, inside],
         out_specs=(hbm, hbm, inside, inside, inside),
         scratch_shapes=[
-            vmem((ROWS, COLS), F32), wide, wide, wide, tall, tall, flat, natural, rows16, rows16, rows16,
+            vmem((ROWS, COLS), F32), wide, wide, wide, tall, flat, natural, rows16, rows16, rows16,
             natural, flat, flat, natural, vmem((2, 8, 2, CA // 2, 128), F32), vmem((2, 8, 2, CA, 128), F32),
             vmem((2, 9, CA, 128), F32), vmem((2, 2, 9, 2, CB, 128), F32), vmem((4, CB, 128), F32),
             vmem((RANK, RANK), F32), small, small, small, small, vmem((NC, 4, 8, RANK), F32),

time: 159 us -> 158 us (level)
  no operation moved by 1% of the time
where the time goes in v7:
time: 158 us; the launch traced here: 157 us
  Pallas kernels  157 us (99%)
    pallas_call x1, Pallas kernels, shards(): pl.pallas_call(functools.partial(factor_kernel, n_cols=n_cols, scale=scal...  152 us
    pallas_call x1, Pallas kernels, shards(): pl.pallas_call(output_kernel, grid=(2,), out_shape=(shape((ROWS, COLS), F...  4.63 us

profile of v7, /device:TPU:1, one launch (start us, length us, event | category | flops | bytes accessed | tf_op | source)
XLA Modules:
  0.0 157.5 jit_solution(374469931660549518)
XLA Ops:
  0.6 152.2 %right_factor.1 = (bf16[3328,256]{1,0:T(8,128)(2,1)}, bf16[3328,256]{1,0:T(8,128)(2,1)}, f32[128,256]{1,0:T(8,128)}, f32[128,256]{1,0:T(8,128)}, f32[52,256]{1,0:T(8,128)}) custom-call(f32[128,3328]{1,0:T(8,128)} %mom.3, bf16[128,3328]{1,0:T(8,128)(2,1)} %grad.3, f32[52,256]{1,0:T(8,128)} %fac.1), custom_call_target="tpu_custom_call" | custom-call | tf_op jit(solution)/shard_map/right_factor/pallas_call | solution.py:542
  152.9 4.6 %outputs.1 = (f32[128,3328]{1,0:T(8,128)}, bf16[128,3328]{1,0:T(8,128)(2,1)}, f32[52,256]{1,0:T(8,128)}) custom-call(f32[128,3328]{1,0:T(8,128)} %mom.3, bf16[128,3328]{1,0:T(8,128)(2,1)} %grad.3, bf16[3328,256]{1,0:T(8,128)(2,1)} %get-tuple-element.8.rfh, bf16[3328,256]{1,0:T(8,128)(2,1)} %get-tuple-element.9.rfl, f32[128,256]{1,0:T(8,128)} %get-tuple-element.10.basis, ...), custom_call_target="tpu_custom_call" | custom-call | tf_op jit(solution)/shard_map/outputs/pallas_call | solution.py:565
